TPU v7x, 32 devices: a whole 2x2x4 slice. The times are simulated.
32 devices in a mesh: ctx: 8 (over z, x), head: 4 (over y, core).
Axes of the slice: x: 2, y: 2, z: 4, core: 2. Of those that a mesh axis runs over, the one named last changes fastest.
Arguments:
- head_input: float32 [2048, 1024], P('ctx', 'head'), may hold values from -6 to 6
- step_size: float32 [16, 2048], P('head', 'ctx'), may hold values from 0.25 to 2
- log_decay: float32 [16, 2048], P('head', 'ctx'), may hold values from -1.6 to 0
- write_proj: float32 [2048, 128], P('ctx'), may hold values from -1.0606601 to 1.0606601
- read_proj: float32 [2048, 128], P('ctx'), may hold values from -0.5 to 0.5
- grad_out: float32 [2048, 1024], P('ctx', 'head'), may hold values from -6 to 6
Outputs:
- head_output: float32 [2048, 1024], P('ctx', 'head')
- grad_input: float32 [2048, 1024], P('ctx', 'head')
- grad_step: float32 [16, 2048], P('head', 'ctx')
- write_grad: float32 [2048, 128], P(('ctx', 'head'))
- read_grad: float32 [2048, 128], P(('ctx', 'head'))
All inputs are finite; a program needn't handle non-finite values.
Results may differ from a plain program's by a relative error of at most 0.00022.
Values sent between devices are 32-bit elements; how exact they have to be, the bound alone decides.
A program may use at most 64 MiB of HBM per device.

v0:
```python
import jax
import jax.numpy as jnp
from jax import lax
from jax.sharding import PartitionSpec as P

GROUP = 128


def prefix(x, axis, combine, identity, reverse):
    size, here = (lax.axis_size(axis), lax.axis_index(axis))
    everything = jax.tree.map(lambda part: lax.all_gather(part, axis), x)
    start = jax.tree.map(
        lambda part, zero: jnp.broadcast_to(jnp.asarray(zero, part.dtype), part.shape), x, identity
    )

    def turn(k, before):
        at = size - 1 - k if reverse else k
        reached = at > here if reverse else at < here
        new = combine(before, jax.tree.map(lambda part: part[at], everything))
        return jax.tree.map(lambda a, b: jnp.where(reached, a, b), new, before)

    return lax.fori_loop(0, size, turn, start)


def combine_forward(first_part, second_part):
    return (
        first_part[0] * second_part[0],
        second_part[1] + second_part[0][:, None, None] * first_part[1],
    )


def combine_backward(first_part, second_part):
    return (
        first_part[0] * second_part[0],
        second_part[1] + second_part[0][:, None, None] * first_part[1],
    )


def shards(head_input, step_size, log_decay, write_proj, read_proj, grad_out):
    highest = lax.Precision.HIGHEST
    head_count = step_size.shape[0]
    row_count = head_input.shape[0]
    head_width = head_input.shape[1] // head_count
    state_width = write_proj.shape[1]
    group_count = row_count // GROUP
    inputs = head_input.reshape(row_count, head_count, head_width).transpose(1, 2, 0)
    scaled = inputs * step_size[:, None, :]
    upstream = grad_out.reshape(row_count, head_count, head_width).transpose(1, 2, 0)
    row_ids = lax.broadcasted_iota(jnp.int32, (GROUP, GROUP), 0)
    col_ids = lax.broadcasted_iota(jnp.int32, (GROUP, GROUP), 1)
    lower_mask = row_ids >= col_ids
    lower_ones = lower_mask.astype(jnp.float32)
    blocks = []
    for position in range(group_count):
        offset = position * GROUP
        group_rates = log_decay[:, offset : offset + GROUP]
        scaled_part = scaled[:, :, offset : offset + GROUP]
        upstream_part = upstream[:, :, offset : offset + GROUP]
        write_part = write_proj[offset : offset + GROUP]
        read_part = read_proj[offset : offset + GROUP]
        cumulated = jnp.dot(group_rates, lower_ones.T, precision=highest)
        final_cum = cumulated[:, -1:]
        gap_logs = cumulated[:, :, None] - cumulated[:, None, :]
        decay_mat = jnp.where(
            lower_mask[None], jnp.exp(jnp.where(lower_mask[None], gap_logs, 0.0)), 0.0
        )
        inner_prod = jnp.dot(read_part, write_part.T, precision=highest)
        mixed_mat = inner_prod[None] * decay_mat
        out_near = jnp.einsum("hts,hps->hpt", mixed_mat, scaled_part, precision=highest)
        back_near = jnp.einsum("hst,hps->hpt", mixed_mat, upstream_part, precision=highest)
        pair_prods = jnp.einsum("hpt,hps->hts", upstream_part, scaled_part, precision=highest)
        weight_sum = jnp.sum(decay_mat * pair_prods, axis=0)
        read_near = jnp.dot(weight_sum, write_part, precision=highest)
        write_near = jnp.dot(weight_sum.T, read_part, precision=highest)
        into_factor = jnp.exp(cumulated)[:, None, :]
        outof_factor = jnp.exp(final_cum - cumulated)[:, None, :]
        whole_decay = jnp.exp(final_cum[:, 0])
        into_upstream = into_factor * upstream_part
        outof_scaled = outof_factor * scaled_part
        fwd_part = jnp.einsum("hps,sn->hpn", outof_scaled, write_part, precision=highest)
        bwd_part = jnp.einsum("hps,sn->hpn", into_upstream, read_part, precision=highest)
        blocks.append(
            (
                into_upstream,
                outof_scaled,
                write_part,
                read_part,
                into_factor,
                outof_factor,
                whole_decay,
                out_near,
                back_near,
                write_near,
                read_near,
                fwd_part,
                bwd_part,
            )
        )
    unit_decay = jnp.ones((head_count,), dtype=jnp.float32)
    zero_state = jnp.zeros((head_count, head_width, state_width), dtype=jnp.float32)
    fwd_decay, fwd_state = (unit_decay, zero_state)
    for entry in blocks:
        fwd_decay = fwd_decay * entry[6]
        fwd_state = entry[6][:, None, None] * fwd_state + entry[11]
    bwd_decay, bwd_state = (unit_decay, zero_state)
    for entry in reversed(blocks):
        bwd_decay = bwd_decay * entry[6]
        bwd_state = entry[12] + entry[6][:, None, None] * bwd_state
    state_in = prefix(
        (fwd_decay, fwd_state), "ctx", combine_forward, (unit_decay, zero_state), False
    )[1]
    grad_in = prefix(
        (bwd_decay, bwd_state), "ctx", combine_backward, (unit_decay, zero_state), True
    )[1]
    entering = []
    current = state_in
    for entry in blocks:
        entering.append(current)
        current = entry[6][:, None, None] * current + entry[11]
    leaving = [None] * group_count
    current = grad_in
    for position in range(group_count - 1, -1, -1):
        leaving[position] = current
        current = blocks[position][12] + blocks[position][6][:, None, None] * current
    out_blocks, back_blocks, write_far, read_far = ([], [], [], [])
    for position in range(group_count):
        into_upstream, outof_scaled, write_part, read_part, into_factor, outof_factor = blocks[
            position
        ][:6]
        state_here = entering[position]
        state_after = leaving[position]
        out_blocks.append(
            blocks[position][7]
            + into_factor * jnp.einsum("tn,hpn->hpt", read_part, state_here, precision=highest)
        )
        back_blocks.append(
            blocks[position][8]
            + outof_factor * jnp.einsum("tn,hpn->hpt", write_part, state_after, precision=highest)
        )
        read_far.append(jnp.einsum("hpt,hpn->tn", into_upstream, state_here, precision=highest))
        write_far.append(jnp.einsum("hpt,hpn->tn", outof_scaled, state_after, precision=highest))
    result_rows = jnp.concatenate(out_blocks, axis=2)
    back_rows = jnp.concatenate(back_blocks, axis=2)
    write_carried = jnp.concatenate(write_far, axis=0)
    read_carried = jnp.concatenate(read_far, axis=0)
    write_total = jnp.concatenate([entry[9] for entry in blocks], axis=0) + write_carried
    read_total = jnp.concatenate([entry[10] for entry in blocks], axis=0) + read_carried
    write_grad, read_grad = (
        lax.psum_scatter(write_total, "head", scatter_dimension=0, tiled=True),
        lax.psum_scatter(read_total, "head", scatter_dimension=0, tiled=True),
    )
    grad_input = (
        (step_size[:, None, :] * back_rows)
        .transpose(2, 0, 1)
        .reshape(row_count, head_count * head_width)
    )
    grad_step = jnp.sum(inputs * back_rows, axis=1)
    head_output = result_rows.transpose(2, 0, 1).reshape(row_count, head_count * head_width)
    return (head_output, grad_input, grad_step, write_grad, read_grad)


def solution(mesh):
    placed = (
        P("ctx", "head"),
        P("head", "ctx"),
        P("head", "ctx"),
        P("ctx", None),
        P("ctx", None),
        P("ctx", "head"),
    )
    return jax.shard_map(
        shards,
        mesh=mesh,
        in_specs=placed,
        out_specs=(
            P("ctx", "head"),
            P("ctx", "head"),
            P("head", "ctx"),
            P(("ctx", "head"), None),
            P(("ctx", "head"), None),
        ),
        check_vma=False,
    )
```

profile of v0, /device:TPU:0, one launch (start us, length us, event | category | flops | bytes accessed | tf_op | source)
XLA Modules:
  0.0 155.9 jit_solution(7166693669869413844)
XLA Ops:
  7.2 0.8 convolution_bitcast_fusion.8
  8.6 1.1 copy.36
  10.0 0.9 convolution_add_fusion.2
  13.1 23.1 %all-reduce = f32[32]{0:T(128)S(1)} all-reduce(f32[32]{0:T(128)S(1)} %dynamic-update-slice), channel_id=3, replica_groups=mesh['ctx'=8,'head'=4] {'ctx'}, use_global_device_ids=true, to_apply=%add | all-reduce | flops 32 | bytes 256
  36.5 0.7 copy-done
  37.7 16.3 %all-gather.8.cloned.1.call-done = f32[32,64,128]{2,1,0:T(8,128)} async-done(((f32[4,64,128]{2,1,0:T(8,128)}), f32[32,64,128]{2,1,0:T(8,128)}) %all-gather.8.cloned.1.call-update) | async-done | bytes 1048592 | tf_op jit(solution)/shard_map/all_gather | solution.py:11
  54.1 8.3 %while.31 = (s32[]{:T(128)}, f32[4,64,128]{2,1,0:T(8,128)S(1)}, s32[]{:T(128)}, f32[8,4,64,128]{3,2,1,0:T(8,128)}, f32[8,4]{1,0:T(8,128)S(1)}, /*index=5*/s32[]{:T(128)}, s32[]{:T(128)}, s32[]{:T(128)}, s32[]{:T(128)}) while((s32[]{:T(128)}, f32[4,64,128]{2,1,0:T(8,128)S(1)}, s32[]{:T(128)}, f32[8,4,64,128]{3,2,1,0:T(8,128)}, ...), condition=%wide.region_3.4_spmd.clone, body=%wide.region_2.3_spmd.clone.sunk | while | flops 131080 | bytes 393439 | solution.py:22
  54.1 1.0 fusion.118
  55.1 1.0 fusion.118
  56.1 1.0 fusion.118
  57.2 1.0 fusion.118
  58.2 1.0 fusion.118
  59.3 1.0 fusion.118
  60.3 1.0 fusion.118
  61.4 1.0 fusion.118
  63.0 0.7 fusion.7
  63.7 0.7 fusion.6
  65.4 0.9 convolution_add_fusion.3
  66.4 0.8 copy.40
  71.0 34.3 %all-gather.6.cloned.1.call-done = f32[32,64,128]{2,1,0:T(8,128)} async-done(((f32[4,64,128]{2,1,0:T(8,128)}), f32[32,64,128]{2,1,0:T(8,128)}) %all-gather.6.cloned.1.call-update) | async-done | bytes 1048592 | tf_op jit(solution)/shard_map/all_gather | solution.py:11
  105.4 8.2 %while.30 = (s32[]{:T(128)}, f32[4,64,128]{2,1,0:T(8,128)S(1)}, s32[]{:T(128)}, f32[8,4,64,128]{3,2,1,0:T(8,128)}, f32[8,4]{1,0:T(8,128)S(1)}, /*index=5*/s32[]{:T(128)}, s32[]{:T(128)}) while((s32[]{:T(128)}, f32[4,64,128]{2,1,0:T(8,128)S(1)}, s32[]{:T(128)}, f32[8,4,64,128]{3,2,1,0:T(8,128)}, f32[8,4]{1,0:T(8,128)S(1)}, ...), condition=%wide.region_1.2_spmd.clone, body=%wide.region_0.1_spmd.clone.sunk | while | flops 131076 | bytes 393377 | solution.py:22
  105.4 1.0 fusion.117
  106.4 1.0 fusion.117
  107.4 1.0 fusion.117
  108.5 1.0 fusion.117
  109.5 1.0 fusion.117
  110.5 1.0 fusion.117
  111.6 1.0 fusion.117
  112.6 1.0 fusion.117
  116.7 0.8 copy.39
  117.5 9.2 %reduce-scatter.3.cloned.1.call-done = f32[64,128]{1,0:T(8,128)} async-done(((f32[256,128]{1,0:T(8,128)}), f32[64,128]{1,0:T(8,128)}) %reduce-scatter.3.cloned.1.call-update) | async-done | bytes 32784 | tf_op jit(solution)/shard_map/reduce_scatter | solution.py:149
  126.8 22.6 %reduce-scatter.5.cloned.1.call-done = f32[64,128]{1,0:T(8,128)} async-done(((f32[256,128]{1,0:T(8,128)}), f32[64,128]{1,0:T(8,128)}) %reduce-scatter.5.cloned.1.call-update) | async-done | bytes 32784 | tf_op jit(solution)/shard_map/reduce_scatter | solution.py:150
  (71 shorter events, 11.6 us)
Async XLA Ops:
  7.2 0.9 copy-start.4
  7.2 46.9 %all-gather.8.cloned.1.call-start = ((), (), s32[]{:S(2)}) async-start(), calls=%async_computation.5 | async-start | bytes 1179648 | tf_op jit(solution)/shard_map/all_gather | solution.py:11
  8.6 1.1 copy-start.1
  10.0 26.3 %copy-start.2 = (f32[256,256]{1,0:T(8,128)S(1)}, f32[256,256]{1,0:T(8,128)}, u32[]{:S(2)}) copy-start(f32[256,256]{1,0:T(8,128)} %param.10) | copy-start | bytes 786436
  10.9 94.4 %all-gather.6.cloned.1.call-start = ((), (), s32[]{:S(2)}) async-start(), calls=%async_computation.4 | async-start | bytes 1179648 | tf_op jit(solution)/shard_map/all_gather | solution.py:11
  11.0 0.7 copy-start.5
  36.3 0.9 copy-start
  63.7 0.7 copy-start.3
  66.3 60.4 %reduce-scatter.3.cloned.1.call-start = ((), (), s32[]{:S(2)}) async-start(), calls=%async_computation.2 | async-start | bytes 163840 | tf_op jit(solution)/shard_map/reduce_scatter | solution.py:149
  71.0 78.4 %reduce-scatter.5.cloned.1.call-start = ((), (), s32[]{:S(2)}) async-start(), calls=%async_computation.3 | async-start | bytes 163840 | tf_op jit(solution)/shard_map/reduce_scatter | solution.py:150
Sparse Core Ops, SparseCore 0:
  11.0 42.9 all-gather.7
  66.4 38.8 all-gather.5
  108.4 18.3 reduce-scatter.2
  129.7 19.5 reduce-scatter.4
where the time goes:
time: 156 us
  waiting for transfers between devices  82.5 us (53%)
  blocking collectives  23.1 us (15%)
  other arithmetic  18.3 us (12%)
  between operations  14.7 us (9%)
  matrix products  11.2 us (7%)
  local copies, waits for them, and re-layouts  5.38 us (3%)
    all_gather x2, waiting for transfers between devices, prefix(): everything = jax.tree.map(lambda part: lax.all_gather(part, axis), x)  50.7 us
    unnamed x1, blocking collectives  23.1 us
    reduce_scatter x1, waiting for transfers between devices, shards(): lax.psum_scatter(read_total, 'head', scatter_dimension=0, tiled=True)  22.6 us
    select_n x16, other arithmetic, turn(): return jax.tree.map(lambda a, b: jnp.where(reached, a, b), new, before)  15.9 us
    reduce_scatter x1, waiting for transfers between devices, shards(): lax.psum_scatter(write_total, 'head', scatter_dimension=0, tiled=True)  9.23 us
    unnamed x19, local copies, waits for them, and re-layouts  5.18 us
  transfers between devices with their start and end apart: 4, of which 4 were waited for; matrix products, arithmetic and copies ran while one was open for 12% of the time, Pallas kernels for 0%

commit v1 on v0

v1 whole, which is shorter than its diff:
```python
import functools

import jax
import jax.numpy as jnp
from jax import lax
from jax.experimental import pallas as pl
from jax.experimental.pallas import tpu as pltpu
from jax.sharding import PartitionSpec as P

MESH = pl.DeviceIdType.MESH
F32 = jnp.float32
BF16 = jnp.bfloat16
HIGHEST = lax.Precision.HIGHEST
PAD = 8


def split(x):
    high = x.astype(BF16)
    return high, (x - high.astype(F32)).astype(BF16)


def dot3(a, b, ca, cb):
    dims = (((ca,), (cb,)), ((), ()))
    dot = functools.partial(lax.dot_general, dimension_numbers=dims, preferred_element_type=F32)
    return dot(a[0], b[0]) + (dot(a[0], b[1]) + dot(a[1], b[0]))


def exact(a, b, ca, cb):
    dims = (((ca,), (cb,)), ((), ()))
    return lax.dot_general(a, b, dims, precision=HIGHEST, preferred_element_type=F32)


def kernel(
    n, nh,
    x_ref, step_ref, log_ref, b_ref, c_ref, g_ref,
    out_ref, gin_ref, gstep_ref, wg_ref, rg_ref,
    st, r1, tz, zbuf, fsend, fs, tot, rs, wsum, back,
    s1_send, s1_recv, z_send, z_recv, s3_send, s3_recv, h_send, h_recv,
):
    tokens, channels = x_ref.shape
    heads = step_ref.shape[0]
    width = channels // heads
    state = b_ref.shape[1]
    half = channels // 2
    half_heads = heads // 2
    m = n // 2
    ck = tokens // nh

    ctx, head = lax.axis_index("ctx"), lax.axis_index("head")
    side, row = lax.rem(ctx, 2), lax.div(ctx, 2)
    partner = row * 2 + (1 - side)

    barrier = pltpu.get_barrier_semaphore()
    pl.semaphore_signal(barrier, inc=1, device_id=(partner, head), device_id_type=MESH)
    for k in range(1, m):
        peer = lax.rem(row + k, m) * 2 + side
        pl.semaphore_signal(barrier, inc=1, device_id=(peer, head), device_id_type=MESH)
    for k in range(1, nh):
        pl.semaphore_signal(
            barrier, inc=1, device_id=(ctx, lax.rem(head + k, nh)), device_id_type=MESH
        )

    mid = tokens // 2
    t_ids = lax.broadcasted_iota(jnp.int32, (tokens, tokens), 0)
    s_ids = lax.broadcasted_iota(jnp.int32, (tokens, tokens), 1)
    lower = t_ids >= s_ids
    weights = jnp.where(
        lower & (s_ids >= mid), 1.0, jnp.where((s_ids > t_ids) & (s_ids < mid), -1.0, 0.0)
    ).astype(F32)
    logs = log_ref[...]
    rel = exact(logs, weights, 1, 1)
    before = jnp.sum(logs[:, :mid], axis=1, keepdims=True)
    last = rel[:, tokens - 1 : tokens]
    into = jnp.exp(rel + before)
    outof = jnp.exp(last - rel)
    total = jnp.exp(last + before)
    cols = jnp.concatenate([step_ref[...], into, outof, rel], axis=0).T
    pick_row = lax.broadcasted_iota(jnp.int32, (4 * heads, 3 * channels), 0)
    pick_col = lax.broadcasted_iota(jnp.int32, (4 * heads, 3 * channels), 1)
    expand = (pick_col // width == pick_row).astype(F32)
    wide = exact(cols, expand, 1, 0)
    step_w = wide[:, :channels]
    into_w = wide[:, channels : 2 * channels]
    outof_w = wide[:, 2 * channels :]

    grads = g_ref[...]
    scaled = x_ref[...] * step_w
    into_g = split(into_w * grads)
    outof_s = split(outof_w * scaled)
    write, read = split(b_ref[...]), split(c_ref[...])
    fwd = dot3(outof_s, write, 0, 0)
    bwd = dot3(into_g, read, 0, 0)
    for j in range(2):
        decay_rows = jnp.broadcast_to(
            total[j * half_heads : (j + 1) * half_heads], (half_heads, state)
        )
        decay_rows = jnp.concatenate([decay_rows] * (PAD // half_heads), axis=0)
        for d, whole in enumerate((fwd, bwd)):
            st[j, d, :half] = whole[j * half : (j + 1) * half]
            st[j, d, half:] = decay_rows

    def widen(rows):
        return jnp.concatenate(
            [jnp.broadcast_to(rows[i : i + 1], (width, state)) for i in range(half_heads)], axis=0
        )

    pl.semaphore_wait(barrier, 1 + (m - 1) + (nh - 1))
    first_copy = pltpu.make_async_remote_copy(
        st.at[1 - side], r1, s1_send, s1_recv, device_id=(partner, head), device_id_type=MESH
    )
    first_copy.start()

    scaled_2, grads_2 = split(scaled), split(grads)
    inner = dot3(read, write, 1, 1)
    lane = lax.broadcasted_iota(jnp.int32, (tokens, channels), 1) // width

    def near(h):
        gap = cols[:, 3 * heads + h : 3 * heads + h + 1] - rel[h : h + 1, :]
        decay = jnp.where(lower, jnp.exp(jnp.where(lower, gap, 0.0)), 0.0)
        mixed = split(inner * decay)
        mine = lane == h

        def only(pair):
            return tuple(jnp.where(mine, part.astype(F32), 0.0).astype(BF16) for part in pair)

        scaled_h, grads_h = only(scaled_2), only(grads_2)
        out_h = dot3(mixed, scaled_h, 1, 0)
        back_h = dot3(mixed, grads_h, 0, 0)
        pair_h = decay * dot3(grads_2, scaled_h, 1, 1)
        if h == 0:
            out_ref[...] = out_h
            back[...] = back_h
            wsum[...] = pair_h
        else:
            out_ref[...] += out_h
            back[...] += back_h
            wsum[...] += pair_h

    near(0)
    first_copy.wait()

    own, other = st[side], r1[...]
    is_first = side == 0
    part_0 = jnp.where(is_first, own, other)
    part_1 = jnp.where(is_first, other, own)
    decay_0, decay_1 = part_0[0, half:], part_1[0, half:]
    wide_0, wide_1 = widen(decay_0), widen(decay_1)
    fwd_0, fwd_1 = part_0[0, :half], part_1[0, :half]
    bwd_0, bwd_1 = part_0[1, :half], part_1[1, :half]
    tz[0, :half] = wide_1 * fwd_0 + fwd_1
    tz[1, :half] = bwd_0 + wide_0 * bwd_1
    for d in range(2):
        tz[d, half:] = decay_0 * decay_1

    z_copies = []
    for k in range(1, m):
        peer_row = lax.rem(row + k, m)
        direction = jnp.where(peer_row > row, 0, 1)
        copy = pltpu.make_async_remote_copy(
            tz.at[direction], zbuf.at[row], z_send.at[k - 1], z_recv.at[row],
            device_id=(peer_row * 2 + side, head), device_id_type=MESH,
        )
        copy.start()
        z_copies.append(copy)

    for h in range(1, heads - 1):
        near(h)

    def joined(j, carried):
        pltpu.make_async_remote_copy(
            tz.at[0], zbuf.at[j], z_send.at[0], z_recv.at[j],
            device_id=(partner, head), device_id_type=MESH,
        ).wait_recv()
        arrived = zbuf[j]
        return arrived[:half] + widen(arrived[half:]) * carried

    zero = jnp.zeros((half, state), F32)
    carry_f = lax.fori_loop(0, row, joined, zero)
    carry_b = lax.fori_loop(0, m - 1 - row, lambda i, c: joined(m - 1 - i, c), zero)

    enter_f = (carry_f, wide_0 * carry_f + fwd_0)
    enter_b = (bwd_1 + wide_1 * carry_b, carry_b)
    for d, pair in enumerate((enter_f, enter_b)):
        fs[side, d] = jnp.where(is_first, pair[0], pair[1])
        fsend[d] = jnp.where(is_first, pair[1], pair[0])
    last_copy = pltpu.make_async_remote_copy(
        fsend, fs.at[side], s3_send, s3_recv, device_id=(partner, head), device_id_type=MESH
    )
    last_copy.start()

    near(heads - 1)
    sums = split(wsum[...])
    read_near = dot3(sums, write, 1, 0)
    write_near = dot3(sums, read, 0, 0)
    last_copy.wait()

    state_f = split(jnp.concatenate([fs[0, 0], fs[1, 0]], axis=0))
    state_b = split(jnp.concatenate([fs[0, 1], fs[1, 1]], axis=0))
    write_all = write_near + dot3(outof_s, state_b, 1, 0)
    read_all = read_near + dot3(into_g, state_f, 1, 0)
    for j in range(nh):
        tot[j, :ck] = write_all[j * ck : (j + 1) * ck]
        tot[j, ck:] = read_all[j * ck : (j + 1) * ck]
    h_copies = []
    for k in range(1, nh):
        peer = lax.rem(head + k, nh)
        copy = pltpu.make_async_remote_copy(
            tot.at[peer], rs.at[k - 1], h_send.at[k - 1], h_recv.at[k - 1],
            device_id=(ctx, peer), device_id_type=MESH,
        )
        copy.start()
        h_copies.append(copy)

    out_ref[...] += into_w * dot3(read, state_f, 1, 1)
    back_all = back[...] + outof_w * dot3(write, state_b, 1, 1)
    gin_ref[...] = step_w * back_all
    sum_row = lax.broadcasted_iota(jnp.int32, (heads, channels), 0)
    sum_col = lax.broadcasted_iota(jnp.int32, (heads, channels), 1)
    gstep_ref[...] = exact((sum_col // width == sum_row).astype(F32), x_ref[...] * back_all, 1, 1)

    result = tot[head]
    for k, copy in enumerate(h_copies):
        copy.wait()
        result = result + rs[k]
    wg_ref[...] = result[:ck]
    rg_ref[...] = result[ck:]
    for copy in z_copies:
        copy.wait_send()


def solution(mesh):
    n, nh = mesh.shape["ctx"], mesh.shape["head"]
    m = n // 2

    def shards(head_input, step_size, log_decay, write_proj, read_proj, grad_out):
        tokens, channels = head_input.shape
        heads = step_size.shape[0]
        state = write_proj.shape[1]
        half, ck = channels // 2, tokens // nh
        vmem = pl.BlockSpec(memory_space=pltpu.VMEM)
        dma = pltpu.SemaphoreType.DMA
        return pl.pallas_call(
            functools.partial(kernel, n, nh),
            out_shape=(
                jax.ShapeDtypeStruct((tokens, channels), F32),
                jax.ShapeDtypeStruct((tokens, channels), F32),
                jax.ShapeDtypeStruct((heads, tokens), F32),
                jax.ShapeDtypeStruct((ck, state), F32),
                jax.ShapeDtypeStruct((ck, state), F32),
            ),
            in_specs=[vmem] * 6,
            out_specs=(vmem,) * 5,
            scratch_shapes=[
                pltpu.VMEM((2, 2, half + PAD, state), F32),
                pltpu.VMEM((2, half + PAD, state), F32),
                pltpu.VMEM((2, half + PAD, state), F32),
                pltpu.VMEM((m, half + PAD, state), F32),
                pltpu.VMEM((2, half, state), F32),
                pltpu.VMEM((2, 2, half, state), F32),
                pltpu.VMEM((nh, 2 * ck, state), F32),
                pltpu.VMEM((nh - 1, 2 * ck, state), F32),
                pltpu.VMEM((tokens, tokens), F32),
                pltpu.VMEM((tokens, channels), F32),
                dma, dma, dma((m - 1,)), dma((m,)), dma, dma, dma((nh - 1,)), dma((nh - 1,)),
            ],
            compiler_params=pltpu.CompilerParams(
                collective_id=0, has_side_effects=True, vmem_limit_bytes=40 * 2**20
            ),
        )(head_input, step_size, log_decay, write_proj, read_proj, grad_out)

    return jax.shard_map(
        shards,
        mesh=mesh,
        in_specs=(
            P("ctx", "head"), P("head", "ctx"), P("head", "ctx"),
            P("ctx", None), P("ctx", None), P("ctx", "head"),
        ),
        out_specs=(
            P("ctx", "head"), P("ctx", "head"), P("head", "ctx"),
            P(("ctx", "head"), None), P(("ctx", "head"), None),
        ),
        check_vma=False,
    )
```

time: 156 us -> 34.7 us (0.22)
  waiting for transfers between devices: 82.5 us -> 0 us
  Pallas kernels: 0 us -> 25.4 us
  blocking collectives: 23.1 us -> 0 us
  other arithmetic: 18.3 us -> 0 us
  between operations: 14.7 us -> 0.66 us
  matrix products: 11.2 us -> 0 us
  local copies, waits for them, and re-layouts: 5.38 us -> 8.3 us
    all_gather x2 -> x0, waiting for transfers between devices: 50.7 us -> none  [prefix(): everything = jax.tree.map(lambda part: lax.all_gather(part, axis), x)]
    reduce_scatter x2 -> x0, waiting for transfers between devices: 31.8 us -> none  [the longest x1 22.6 us: shards(): lax.psum_scatter(read_total, 'head', scatter_dimension=0, tiled=True)]
    pallas_call x0 -> x1, Pallas kernels: none -> 25.4 us  [shards(): pl.pallas_call(functools.partial(kernel, n, nh), out_shape=(jax.ShapeDtyp...]
    unnamed x1 -> x0, blocking collectives: 23.1 us -> none
    select_n x16 -> x0, other arithmetic: 15.9 us -> none  [turn(): return jax.tree.map(lambda a, b: jnp.where(reached, a, b), new, before)]
    dot_general x26 -> x0, matrix products: 11.2 us -> none  [the longest x2 1.42 us: shards(): jnp.einsum('hst,hps->hpt', mixed_mat, upstream_part, precision=highest)]
    unnamed x19 -> x17, local copies, waits for them, and re-layouts: 5.18 us -> 8.3 us
  transfers between devices with their start and end apart: 4 -> 0, of which waited for: 4 -> 0; matrix products, arithmetic and copies ran while one was open for 12% -> 0% of each run, Pallas kernels for 0% -> 0%
where the time goes in v1:
time: 34.7 us; the launch traced here: 34.3 us
  Pallas kernels  25.4 us (73%)
  local copies, waits for them, and re-layouts  8.3 us (24%)
  between operations  0.66 us (2%)
    pallas_call x1, Pallas kernels, shards(): pl.pallas_call(functools.partial(kernel, n, nh), out_shape=(jax.ShapeDtyp...  25.4 us
    unnamed x17, local copies, waits for them, and re-layouts  8.3 us

profile of v1, /device:TPU:0, one launch (start us, length us, event | category | flops | bytes accessed | tf_op | source)
XLA Modules:
  0.0 34.3 jit_solution(8371258172544772988)
XLA Ops:
  0.6 0.0 copy-start
  0.6 0.9 %copy-done = f32[256,256]{1,0:T(8,128)S(1)} copy-done((f32[256,256]{1,0:T(8,128)S(1)}, f32[256,256]{1,0:T(8,128)}, u32[]{:S(2)}) %copy-start) | copy-done | bytes 262168
  1.6 0.0 copy-start.1
  1.6 0.9 %copy-done.1 = f32[256,256]{1,0:T(8,128)S(1)} copy-done((f32[256,256]{1,0:T(8,128)S(1)}, f32[256,256]{1,0:T(8,128)}, u32[]{:S(2)}) %copy-start.1) | copy-done | bytes 262168
  2.5 0.0 copy-start.2
  2.5 0.9 %copy-done.2 = f32[256,128]{1,0:T(8,128)S(1)} copy-done((f32[256,128]{1,0:T(8,128)S(1)}, f32[256,128]{1,0:T(8,128)}, u32[]{:S(2)}) %copy-start.2) | copy-done | bytes 131096
  3.4 0.0 copy-start.3
  3.4 0.9 %copy-done.3 = f32[256,128]{1,0:T(8,128)S(1)} copy-done((f32[256,128]{1,0:T(8,128)S(1)}, f32[256,128]{1,0:T(8,128)}, u32[]{:S(2)}) %copy-start.3) | copy-done | bytes 131096
  4.3 0.0 copy-start.4
  4.3 0.7 %copy-done.4 = f32[4,256]{1,0:T(4,128)S(1)} copy-done((f32[4,256]{1,0:T(4,128)S(1)}, f32[4,256]{1,0:T(4,128)}, u32[]{:S(2)}) %copy-start.4) | copy-done | bytes 4120
  5.0 0.0 copy-start.5
  5.0 0.7 %copy-done.5 = f32[4,256]{1,0:T(4,128)S(1)} copy-done((f32[4,256]{1,0:T(4,128)S(1)}, f32[4,256]{1,0:T(4,128)}, u32[]{:S(2)}) %copy-start.5) | copy-done | bytes 4120
  5.7 25.4 %shard_map.101 = (f32[256,256]{1,0:T(8,128)S(1)}, f32[256,256]{1,0:T(8,128)S(1)}, f32[4,256]{1,0:T(4,128)S(1)}, f32[64,128]{1,0:T(8,128)S(1)}, f32[64,128]{1,0:T(8,128)S(1)}) custom-call(f32[256,256]{1,0:T(8,128)S(1)} %copy-done, f32[4,256]{1,0:T(4,128)S(1)} %copy-done.4, f32[4,256]{1,0:T(4,128)S(1)} %copy-done.5, f32[256,128]{1,0:T(8,128)S(1)} %copy-done.2, ...), custom_call_target="tpu_custom_call" | custom-call | tf_op jit(solution)/shard_map/pallas_call | solution.py:242
  31.1 0.7 %copy.16 = f32[256,256]{1,0:T(8,128)} copy(f32[256,256]{1,0:T(8,128)S(1)} %get-tuple-element.10) | data formatting | bytes 524288
  31.8 0.7 %copy.17 = f32[256,256]{1,0:T(8,128)} copy(f32[256,256]{1,0:T(8,128)S(1)} %get-tuple-element.11) | data formatting | bytes 524288
  32.5 0.6 %copy.18 = f32[4,256]{1,0:T(4,128)} copy(f32[4,256]{1,0:T(4,128)S(1)} %get-tuple-element.12) | data formatting | bytes 8192
  33.1 0.6 %copy.19 = f32[64,128]{1,0:T(8,128)} copy(f32[64,128]{1,0:T(8,128)S(1)} %get-tuple-element.13) | data formatting | bytes 65536
  33.7 0.6 %copy.20 = f32[64,128]{1,0:T(8,128)} copy(f32[64,128]{1,0:T(8,128)S(1)} %get-tuple-element.14) | data formatting | bytes 65536
Async XLA Ops:
  0.6 1.0 %copy-start = (f32[256,256]{1,0:T(8,128)S(1)}, f32[256,256]{1,0:T(8,128)}, u32[]{:S(2)}) copy-start(f32[256,256]{1,0:T(8,128)} %x_ref.1) | copy-start | bytes 786436
  1.6 0.9 %copy-start.1 = (f32[256,256]{1,0:T(8,128)S(1)}, f32[256,256]{1,0:T(8,128)}, u32[]{:S(2)}) copy-start(f32[256,256]{1,0:T(8,128)} %g_ref.1) | copy-start | bytes 786436
  2.5 0.9 %copy-start.2 = (f32[256,128]{1,0:T(8,128)S(1)}, f32[256,128]{1,0:T(8,128)}, u32[]{:S(2)}) copy-start(f32[256,128]{1,0:T(8,128)} %b_ref.1) | copy-start | bytes 393220
  3.4 0.9 %copy-start.3 = (f32[256,128]{1,0:T(8,128)S(1)}, f32[256,128]{1,0:T(8,128)}, u32[]{:S(2)}) copy-start(f32[256,128]{1,0:T(8,128)} %c_ref.1) | copy-start | bytes 393220
  4.3 0.7 %copy-start.4 = (f32[4,256]{1,0:T(4,128)S(1)}, f32[4,256]{1,0:T(4,128)}, u32[]{:S(2)}) copy-start(f32[4,256]{1,0:T(4,128)} %step_ref.1) | copy-start | bytes 12292
  5.0 0.7 %copy-start.5 = (f32[4,256]{1,0:T(4,128)S(1)}, f32[4,256]{1,0:T(4,128)}, u32[]{:S(2)}) copy-start(f32[4,256]{1,0:T(4,128)} %log_ref.1) | copy-start | bytes 12292

commit v2 on v1

v2 whole, which is shorter than its diff:
```python
import functools

import jax
import jax.numpy as jnp
from jax import lax
from jax.experimental import pallas as pl
from jax.experimental.pallas import tpu as pltpu
from jax.sharding import PartitionSpec as P

MESH = pl.DeviceIdType.MESH
F32 = jnp.float32
BF16 = jnp.bfloat16
PAD = 8
GRANT = 60 * 2**20
CHUNKS = 2


def split(x):
    high = x.astype(BF16)
    return high, (x - high.astype(F32)).astype(BF16)


def dot3(a, b, ca, cb):
    dims = (((ca,), (cb,)), ((), ()))
    dot = functools.partial(lax.dot_general, dimension_numbers=dims, preferred_element_type=F32)
    return dot(a[0], b[0]) + (dot(a[0], b[1]) + dot(a[1], b[0]))


def thirds(rows):
    zeros = jnp.zeros((16 - rows.shape[0], rows.shape[1]), F32)
    pieces = []
    for _ in range(3):
        piece = rows.astype(BF16)
        rows = rows - piece.astype(F32)
        pieces.append(jnp.concatenate([piece.astype(F32), zeros], axis=0))
    return jnp.concatenate(pieces, axis=0).astype(BF16)


def kernel(
    n, nh,
    x_hbm, step_hbm, log_hbm, b_hbm, c_hbm, g_hbm,
    out_hbm, gin_hbm, gstep_hbm, wg_hbm, rg_hbm,
    x_ref, step_ref, log_ref, b_ref, c_ref, g_ref,
    out_ref, gin_ref, gstep_ref, wg_ref, rg_ref,
    st, r1, tz, zbuf, fsend, fs, tot, rs, wsum, back,
    in_sem, out_sem, s1_send, s1_recv, z_send, z_recv, s3_send, s3_recv, h_send, h_recv,
):
    tokens, channels = x_ref.shape
    heads = step_ref.shape[0]
    width = channels // heads
    state = b_ref.shape[1]
    half = channels // 2
    m = n // 2
    ck = tokens // nh
    piece = state // CHUNKS

    ctx, head = lax.axis_index("ctx"), lax.axis_index("head")
    side, row = lax.rem(ctx, 2), lax.div(ctx, 2)
    partner = row * 2 + (1 - side)

    barrier = pltpu.get_barrier_semaphore()
    pl.semaphore_signal(barrier, inc=1, device_id=(partner, head), device_id_type=MESH)
    for k in range(1, m):
        peer = lax.rem(row + k, m) * 2 + side
        pl.semaphore_signal(barrier, inc=1, device_id=(peer, head), device_id_type=MESH)
    for k in range(1, nh):
        pl.semaphore_signal(
            barrier, inc=1, device_id=(ctx, lax.rem(head + k, nh)), device_id_type=MESH
        )

    loads = [
        pltpu.make_async_copy(source, target, in_sem.at[i])
        for i, (source, target) in enumerate((
            (log_hbm, log_ref), (step_hbm, step_ref), (b_hbm, b_ref),
            (c_hbm, c_ref), (x_hbm, x_ref), (g_hbm, g_ref),
        ))
    ]
    for load in loads:
        load.start()

    stores = [
        pltpu.make_async_copy(source, target, out_sem.at[i])
        for i, (source, target) in enumerate((
            (out_ref, out_hbm), (gin_ref, gin_hbm), (gstep_ref, gstep_hbm),
            (wg_ref, wg_hbm), (rg_ref, rg_hbm),
        ))
    ]

    mid = tokens // 2
    row_ids = lax.broadcasted_iota(jnp.int32, (tokens, tokens), 0)
    col_ids = lax.broadcasted_iota(jnp.int32, (tokens, tokens), 1)
    weights = jnp.where(
        (row_ids <= col_ids) & (row_ids >= mid),
        1.0,
        jnp.where((row_ids > col_ids) & (row_ids < mid), -1.0, 0.0),
    ).astype(BF16)
    pick_row = lax.broadcasted_iota(jnp.int32, (48, 3 * channels), 0) % 16
    pick_col = lax.broadcasted_iota(jnp.int32, (48, 3 * channels), 1) // width
    expand = jnp.where(pick_row == pick_col, 1.0, 0.0).astype(BF16)

    loads[0].wait()
    logs = log_ref[...]
    sums = jnp.dot(thirds(logs), weights, preferred_element_type=F32)
    rel = sums[:heads] + sums[16 : 16 + heads] + sums[32 : 32 + heads]
    before = jnp.sum(logs[:, :mid], axis=1, keepdims=True)
    last = rel[:, tokens - 1 : tokens]
    into = jnp.exp(rel + before)
    outof = jnp.exp(last - rel)
    loads[1].wait()
    factors = thirds(jnp.concatenate([step_ref[...], into, outof], axis=0))
    wide = lax.dot_general(
        factors, expand, (((0,), (0,)), ((), ())), preferred_element_type=F32
    )
    step_w = wide[:, :channels]
    into_w = wide[:, channels : 2 * channels]
    outof_w = wide[:, 2 * channels :]

    loads[2].wait()
    write, write_t = split(b_ref[...]), split(b_ref[...].T)
    loads[3].wait()
    read, read_t = split(c_ref[...]), split(c_ref[...].T)
    loads[4].wait()
    scaled = x_ref[...] * step_w
    outof_s = split(outof_w * scaled)
    fwd = dot3(write_t, outof_s, 1, 0)
    loads[5].wait()
    grads = g_ref[...]
    into_g = split(into_w * grads)
    bwd = dot3(read_t, into_g, 1, 0)
    decay_rows = jnp.broadcast_to(into_w[tokens - 1 : tokens], (PAD, channels))
    for j in range(2):
        for d, whole in enumerate((fwd, bwd)):
            st[j, d, :PAD] = decay_rows[:, j * half : (j + 1) * half]
            st[j, d, PAD:] = whole[:, j * half : (j + 1) * half]

    def span(i):
        return pl.ds(0, PAD + piece) if i == 0 else pl.ds(PAD + i * piece, piece)

    def spread(decay):
        return jnp.concatenate([decay] * (piece // PAD), axis=0)

    pl.semaphore_wait(barrier, 1 + (m - 1) + (nh - 1))
    first_copies = [
        pltpu.make_async_remote_copy(
            st.at[1 - side, :, span(i)], r1.at[:, span(i)], s1_send.at[i], s1_recv.at[i],
            device_id=(partner, head), device_id_type=MESH,
        )
        for i in range(CHUNKS)
    ]
    for copy in first_copies:
        copy.start()

    scaled_2, grads_2 = split(scaled), split(grads)
    inner = dot3(read, write_t, 1, 0)
    lane = lax.broadcasted_iota(jnp.int32, (tokens, channels), 1) // width
    rel_cols = jnp.concatenate([rel] * (8 // heads), axis=0).T
    lower = row_ids >= col_ids

    def near(h):
        gap = rel_cols[:, h : h + 1] - rel[h : h + 1, :]
        decay = jnp.where(lower, jnp.exp(jnp.where(lower, gap, 0.0)), 0.0)
        mixed = split(inner * decay)
        mine = lane == h

        def only(pair):
            return tuple(jnp.where(mine, part.astype(F32), 0.0).astype(BF16) for part in pair)

        scaled_h, grads_h = only(scaled_2), only(grads_2)
        out_h = dot3(mixed, scaled_h, 1, 0)
        back_h = dot3(mixed, grads_h, 0, 0)
        pair_h = decay * dot3(grads_2, scaled_h, 1, 1)
        if h == 0:
            out_ref[...] = out_h
            back[...] = back_h
            wsum[...] = pair_h
        else:
            out_ref[...] += out_h
            back[...] += back_h
            wsum[...] += pair_h

    is_first = side == 0

    def rows_of(i):
        return slice(PAD + i * piece, PAD + (i + 1) * piece)

    def pair_parts(i):
        own, other = st[side, :, rows_of(i)], r1[:, rows_of(i)]
        own_decay, other_decay = st[side, 0, :PAD], r1[0, :PAD]
        return (
            jnp.where(is_first, own, other),
            jnp.where(is_first, other, own),
            spread(jnp.where(is_first, own_decay, other_decay)),
            spread(jnp.where(is_first, other_decay, own_decay)),
        )

    z_copies = []

    def send_totals(i):
        first_copies[i].wait()
        part_0, part_1, decay_0, decay_1 = pair_parts(i)
        tz[0, rows_of(i)] = decay_1 * part_0[0] + part_1[0]
        tz[1, rows_of(i)] = part_0[1] + decay_0 * part_1[1]
        if i == 0:
            for d in range(2):
                tz[d, :PAD] = decay_0[:PAD] * decay_1[:PAD]
        for k in range(1, m):
            peer_row = lax.rem(row + k, m)
            direction = jnp.where(peer_row > row, 0, 1)
            copy = pltpu.make_async_remote_copy(
                tz.at[direction, span(i)], zbuf.at[row, span(i)],
                z_send.at[i, k - 1], z_recv.at[i, row],
                device_id=(peer_row * 2 + side, head), device_id_type=MESH,
            )
            copy.start()
            z_copies.append(copy)

    last_copies = []

    def send_entering(i):
        def joined(j, carried):
            pltpu.make_async_remote_copy(
                tz.at[0, span(i)], zbuf.at[j, span(i)], z_send.at[i, 0], z_recv.at[i, j],
                device_id=(partner, head), device_id_type=MESH,
            ).wait_recv()
            return zbuf[j, rows_of(i)] + spread(zbuf[j, :PAD]) * carried

        zero = jnp.zeros((piece, half), F32)
        carry_f = lax.fori_loop(0, row, joined, zero)
        carry_b = lax.fori_loop(0, m - 1 - row, lambda k, c: joined(m - 1 - k, c), zero)
        part_0, part_1, decay_0, decay_1 = pair_parts(i)
        enter_f = (carry_f, decay_0 * carry_f + part_0[0])
        enter_b = (part_1[1] + decay_1 * carry_b, carry_b)
        for d, pair in enumerate((enter_f, enter_b)):
            fs[side, d, i * piece : (i + 1) * piece] = jnp.where(is_first, pair[0], pair[1])
            fsend[d, i * piece : (i + 1) * piece] = jnp.where(is_first, pair[1], pair[0])
        here = pl.ds(i * piece, piece)
        copy = pltpu.make_async_remote_copy(
            fsend.at[:, here], fs.at[side, :, here], s3_send.at[i], s3_recv.at[i],
            device_id=(partner, head), device_id_type=MESH,
        )
        copy.start()
        last_copies.append(copy)

    near(0)
    send_totals(0)
    near(1)
    for i in range(1, CHUNKS):
        send_totals(i)
    near(2)
    send_entering(0)
    near(3)
    mixed_sums = split(wsum[...])
    read_near = dot3(mixed_sums, write, 1, 0)
    write_near = dot3(mixed_sums, read, 0, 0)
    for i in range(1, CHUNKS):
        send_entering(i)
    for copy in last_copies:
        copy.wait()

    state_f = split(jnp.concatenate([fs[0, 0], fs[1, 0]], axis=1))
    state_b = split(jnp.concatenate([fs[0, 1], fs[1, 1]], axis=1))
    write_all = write_near + dot3(outof_s, state_b, 1, 1)
    read_all = read_near + dot3(into_g, state_f, 1, 1)
    for j in range(nh):
        tot[j, :ck] = write_all[j * ck : (j + 1) * ck]
        tot[j, ck:] = read_all[j * ck : (j + 1) * ck]
    h_copies = []
    for k in range(1, nh):
        peer = lax.rem(head + k, nh)
        copy = pltpu.make_async_remote_copy(
            tot.at[peer], rs.at[k - 1], h_send.at[k - 1], h_recv.at[k - 1],
            device_id=(ctx, peer), device_id_type=MESH,
        )
        copy.start()
        h_copies.append(copy)

    out_ref[...] += into_w * dot3(read, state_f, 1, 0)
    stores[0].start()
    back_all = back[...] + outof_w * dot3(write, state_b, 1, 0)
    gin_ref[...] = step_w * back_all
    stores[1].start()
    pick_row = lax.broadcasted_iota(jnp.int32, (16, channels), 0)
    pick_col = lax.broadcasted_iota(jnp.int32, (16, channels), 1) // width
    pick = jnp.where(pick_row == pick_col, 1.0, 0.0).astype(BF16)
    high, low = split(x_ref[...] * back_all)
    nt = (((1,), (1,)), ((), ()))
    steps = lax.dot_general(pick, high, nt, preferred_element_type=F32) + lax.dot_general(
        pick, low, nt, preferred_element_type=F32
    )
    gstep_ref[...] = steps[:heads]
    stores[2].start()

    result = tot[head]
    for k, copy in enumerate(h_copies):
        copy.wait()
        result = result + rs[k]
    wg_ref[...] = result[:ck]
    stores[3].start()
    rg_ref[...] = result[ck:]
    stores[4].start()
    for copy in z_copies:
        copy.wait_send()
    for store in stores:
        store.wait()


def place(*refs):
    count = len(refs) // 2
    sems = refs[-1]
    copies = [
        pltpu.make_async_copy(refs[i], refs[count + i], sems.at[i]) for i in range(count)
    ]
    for copy in copies:
        copy.start()
    for copy in copies:
        copy.wait()


def solution(mesh):
    n, nh = mesh.shape["ctx"], mesh.shape["head"]
    m = n // 2

    def shards(head_input, step_size, log_decay, write_proj, read_proj, grad_out):
        tokens, channels = head_input.shape
        heads = step_size.shape[0]
        state = write_proj.shape[1]
        half, ck = channels // 2, tokens // nh
        hbm = pl.BlockSpec(memory_space=pltpu.HBM)
        dma = pltpu.SemaphoreType.DMA
        shapes = (
            jax.ShapeDtypeStruct((tokens, channels), F32),
            jax.ShapeDtypeStruct((tokens, channels), F32),
            jax.ShapeDtypeStruct((heads, tokens), F32),
            jax.ShapeDtypeStruct((ck, state), F32),
            jax.ShapeDtypeStruct((ck, state), F32),
        )
        results = pl.pallas_call(
            functools.partial(kernel, n, nh),
            out_shape=shapes,
            in_specs=[hbm] * 6,
            out_specs=(hbm,) * 5,
            scratch_shapes=[
                pltpu.VMEM((tokens, channels), F32),
                pltpu.VMEM((heads, tokens), F32),
                pltpu.VMEM((heads, tokens), F32),
                pltpu.VMEM((tokens, state), F32),
                pltpu.VMEM((tokens, state), F32),
                pltpu.VMEM((tokens, channels), F32),
                *(pltpu.VMEM(shape.shape, F32) for shape in shapes),
                pltpu.VMEM((2, 2, state + PAD, half), F32),
                pltpu.VMEM((2, state + PAD, half), F32),
                pltpu.VMEM((2, state + PAD, half), F32),
                pltpu.VMEM((m, state + PAD, half), F32),
                pltpu.VMEM((2, state, half), F32),
                pltpu.VMEM((2, 2, state, half), F32),
                pltpu.VMEM((nh, 2 * ck, state), F32),
                pltpu.VMEM((nh - 1, 2 * ck, state), F32),
                pltpu.VMEM((tokens, tokens), F32),
                pltpu.VMEM((tokens, channels), F32),
                dma((6,)), dma((5,)),
                dma((CHUNKS,)), dma((CHUNKS,)),
                dma((CHUNKS, m - 1)), dma((CHUNKS, m)),
                dma((CHUNKS,)), dma((CHUNKS,)),
                dma((nh - 1,)), dma((nh - 1,)),
            ],
            compiler_params=pltpu.CompilerParams(
                collective_id=0, has_side_effects=True, vmem_limit_bytes=GRANT
            ),
        )(head_input, step_size, log_decay, write_proj, read_proj, grad_out)
        return pl.pallas_call(
            place,
            out_shape=shapes,
            in_specs=[hbm] * 5,
            out_specs=(hbm,) * 5,
            scratch_shapes=[dma((5,))],
            compiler_params=pltpu.CompilerParams(vmem_limit_bytes=GRANT),
        )(*results)

    return jax.shard_map(
        shards,
        mesh=mesh,
        in_specs=(
            P("ctx", "head"), P("head", "ctx"), P("head", "ctx"),
            P("ctx", None), P("ctx", None), P("ctx", "head"),
        ),
        out_specs=(
            P("ctx", "head"), P("ctx", "head"), P("head", "ctx"),
            P(("ctx", "head"), None), P(("ctx", "head"), None),
        ),
        check_vma=False,
    )
```

time: 34.7 us -> 44.4 us (1.28)
  Pallas kernels: 25.4 us -> 43.5 us
  local copies, waits for them, and re-layouts: 8.3 us -> 0 us
    pallas_call x1 -> x2, Pallas kernels: 25.4 us -> 43.5 us  [the longest x1 24.3 us: shards(): pl.pallas_call(functools.partial(kernel, n, nh), out_shape=shapes, in_spe...]
    unnamed x17 -> x0, local copies, waits for them, and re-layouts: 8.3 us -> none
where the time goes in v2:
time: 44.4 us; the launch traced here: 44.1 us
  Pallas kernels  43.5 us (98%)
  between operations  0.64 us (1%)
    pallas_call x1, Pallas kernels, shards(): pl.pallas_call(functools.partial(kernel, n, nh), out_shape=shapes, in_spe...  24.3 us
    pallas_call x1, Pallas kernels, shards(): pl.pallas_call(place, out_shape=shapes, in_specs=[hbm] * 5, out_specs=(hb...  19.1 us

profile of v2, /device:TPU:0, one launch (start us, length us, event | category | flops | bytes accessed | tf_op | source)
XLA Modules:
  0.0 44.1 jit_solution(13503768117262578449)
XLA Ops:
  0.6 24.3 %shard_map.101 = (f32[256,256]{1,0:T(8,128)}, f32[256,256]{1,0:T(8,128)}, f32[4,256]{1,0:T(4,128)}, f32[64,128]{1,0:T(8,128)}, f32[64,128]{1,0:T(8,128)}) custom-call(f32[256,256]{1,0:T(8,128)} %x_hbm.1, f32[4,256]{1,0:T(4,128)} %step_hbm.1, f32[4,256]{1,0:T(4,128)} %log_hbm.1, f32[256,128]{1,0:T(8,128)} %b_hbm.1, f32[256,128]{1,0:T(8,128)} %c_hbm.1, ...), custom_call_target="tpu_custom_call" | custom-call | tf_op jit(solution)/shard_map/pallas_call | solution.py:337
  25.0 19.1 %shard_map.102 = (f32[256,256]{1,0:T(8,128)}, f32[256,256]{1,0:T(8,128)}, f32[4,256]{1,0:T(4,128)}, f32[64,128]{1,0:T(8,128)}, f32[64,128]{1,0:T(8,128)}) custom-call(f32[256,256]{1,0:T(8,128)} %get-tuple-element.10.refs_0_, f32[256,256]{1,0:T(8,128)} %get-tuple-element.11.refs_1_, f32[4,256]{1,0:T(4,128)} %get-tuple-element.12.refs_2_, ...), custom_call_target="tpu_custom_call" | custom-call | tf_op jit(solution)/shard_map/pallas_call | solution.py:370

commit v3 on v2

--- a/solution.py
+++ b/solution.py
@@ -305,15 +305,18 @@
 
 
 def place(*refs):
-    count = len(refs) // 2
-    sems = refs[-1]
-    copies = [
-        pltpu.make_async_copy(refs[i], refs[count + i], sems.at[i]) for i in range(count)
-    ]
-    for copy in copies:
-        copy.start()
-    for copy in copies:
-        copy.wait()
+    count = (len(refs) - 2) // 3
+    sources, targets, held = refs[:count], refs[count : 2 * count], refs[2 * count : 3 * count]
+    in_sem, out_sem = refs[-2:]
+    loads = [pltpu.make_async_copy(sources[i], held[i], in_sem.at[i]) for i in range(count)]
+    stores = [pltpu.make_async_copy(held[i], targets[i], out_sem.at[i]) for i in range(count)]
+    for load in loads:
+        load.start()
+    for load, store in zip(loads, stores):
+        load.wait()
+        store.start()
+    for store in stores:
+        store.wait()
 
 
 def solution(mesh):
@@ -372,7 +375,9 @@
             out_shape=shapes,
             in_specs=[hbm] * 5,
             out_specs=(hbm,) * 5,
-            scratch_shapes=[dma((5,))],
+            scratch_shapes=[
+                *(pltpu.VMEM(shape.shape, F32) for shape in shapes), dma((5,)), dma((5,)),
+            ],
             compiler_params=pltpu.CompilerParams(vmem_limit_bytes=GRANT),
         )(*results)
 

time: 44.4 us -> 27.1 us (0.61)
  Pallas kernels: 43.5 us -> 26.2 us
    pallas_call x1, Pallas kernels: 19.1 us -> 1.84 us  [shards(): pl.pallas_call(place, out_shape=shapes, in_specs=[hbm] * 5, out_specs=(hb...]
where the time goes in v3:
time: 27.1 us; the launch traced here: 26.8 us
  Pallas kernels  26.2 us (97%)
  between operations  0.64 us (2%)
    pallas_call x1, Pallas kernels, shards(): pl.pallas_call(functools.partial(kernel, n, nh), out_shape=shapes, in_spe...  24.3 us
    pallas_call x1, Pallas kernels, shards(): pl.pallas_call(place, out_shape=shapes, in_specs=[hbm] * 5, out_specs=(hb...  1.84 us

profile of v3, /device:TPU:0, one launch (start us, length us, event | category | flops | bytes accessed | tf_op | source)
XLA Modules:
  0.0 26.8 jit_solution(1045054677932526708)
XLA Ops:
  0.6 24.3 %shard_map.101 = (f32[256,256]{1,0:T(8,128)}, f32[256,256]{1,0:T(8,128)}, f32[4,256]{1,0:T(4,128)}, f32[64,128]{1,0:T(8,128)}, f32[64,128]{1,0:T(8,128)}) custom-call(f32[256,256]{1,0:T(8,128)} %x_hbm.1, f32[4,256]{1,0:T(4,128)} %step_hbm.1, f32[4,256]{1,0:T(4,128)} %log_hbm.1, f32[256,128]{1,0:T(8,128)} %b_hbm.1, f32[256,128]{1,0:T(8,128)} %c_hbm.1, ...), custom_call_target="tpu_custom_call" | custom-call | tf_op jit(solution)/shard_map/pallas_call | solution.py:340
  25.0 1.8 %shard_map.102 = (f32[256,256]{1,0:T(8,128)}, f32[256,256]{1,0:T(8,128)}, f32[4,256]{1,0:T(4,128)}, f32[64,128]{1,0:T(8,128)}, f32[64,128]{1,0:T(8,128)}) custom-call(f32[256,256]{1,0:T(8,128)} %get-tuple-element.10.refs_0_, f32[256,256]{1,0:T(8,128)} %get-tuple-element.11.refs_1_, f32[4,256]{1,0:T(4,128)} %get-tuple-element.12.refs_2_, ...), custom_call_target="tpu_custom_call" | custom-call | tf_op jit(solution)/shard_map/pallas_call | solution.py:373

commit v4 on v3

--- a/solution.py
+++ b/solution.py
@@ -12,7 +12,7 @@
 BF16 = jnp.bfloat16
 PAD = 8
 GRANT = 60 * 2**20
-CHUNKS = 2
+CHUNKS = 4
 
 
 def split(x):
@@ -21,9 +21,9 @@
 
 
 def dot3(a, b, ca, cb):
-    dims = (((ca,), (cb,)), ((), ()))
-    dot = functools.partial(lax.dot_general, dimension_numbers=dims, preferred_element_type=F32)
-    return dot(a[0], b[0]) + (dot(a[0], b[1]) + dot(a[1], b[0]))
+    left = jnp.concatenate([a[0], a[0], a[1]], axis=ca)
+    right = jnp.concatenate([b[0], b[1], b[0]], axis=cb)
+    return lax.dot_general(left, right, (((ca,), (cb,)), ((), ())), preferred_element_type=F32)
 
 
 def thirds(rows):
@@ -151,32 +151,38 @@
         copy.start()
 
     scaled_2, grads_2 = split(scaled), split(grads)
-    inner = dot3(read, write_t, 1, 0)
-    lane = lax.broadcasted_iota(jnp.int32, (tokens, channels), 1) // width
+    panels = ((0, mid), (mid, tokens))
+
+    def part(pair, rows, columns=slice(None)):
+        return tuple(x[rows, columns] for x in pair)
+
+    inner = [
+        dot3(part(read, slice(lo, hi)), part(write_t, slice(None), slice(0, hi)), 1, 0)
+        for lo, hi in panels
+    ]
+    lanes = 2 * width
+    lane = lax.broadcasted_iota(jnp.int32, (1, lanes), 1) // width
     rel_cols = jnp.concatenate([rel] * (8 // heads), axis=0).T
-    lower = row_ids >= col_ids
+    out_ref[...] = jnp.zeros_like(out_ref)
+    back[...] = jnp.zeros_like(back)
+    wsum[...] = jnp.zeros_like(wsum)
 
     def near(h):
-        gap = rel_cols[:, h : h + 1] - rel[h : h + 1, :]
-        decay = jnp.where(lower, jnp.exp(jnp.where(lower, gap, 0.0)), 0.0)
-        mixed = split(inner * decay)
-        mine = lane == h
-
-        def only(pair):
-            return tuple(jnp.where(mine, part.astype(F32), 0.0).astype(BF16) for part in pair)
-
-        scaled_h, grads_h = only(scaled_2), only(grads_2)
-        out_h = dot3(mixed, scaled_h, 1, 0)
-        back_h = dot3(mixed, grads_h, 0, 0)
-        pair_h = decay * dot3(grads_2, scaled_h, 1, 1)
-        if h == 0:
-            out_ref[...] = out_h
-            back[...] = back_h
-            wsum[...] = pair_h
-        else:
-            out_ref[...] += out_h
-            back[...] += back_h
-            wsum[...] += pair_h
+        here = slice(h // 2 * lanes, (h // 2 + 1) * lanes)
+        mask = jnp.where(lane == h % 2, 1.0, 0.0).astype(BF16)
+        scaled_h = tuple(x[:, here] * mask for x in scaled_2)
+        grads_h = tuple(x[:, here] * mask for x in grads_2)
+        for k, (lo, hi) in enumerate(panels):
+            rows, reach = slice(lo, hi), slice(0, hi)
+            gap = rel_cols[rows, h : h + 1] - rel[h : h + 1, reach]
+            lower = row_ids[rows, reach] >= col_ids[rows, reach]
+            decay = jnp.exp(jnp.where(lower, gap, -1e30))
+            mixed = split(inner[k] * decay)
+            out_ref[rows, here] += dot3(mixed, part(scaled_h, reach), 1, 0)
+            back[reach, here] += dot3(mixed, part(grads_h, rows), 0, 0)
+            wsum[rows, reach] += decay * dot3(
+                part(grads_2, rows, here), part(scaled_h, reach), 1, 1
+            )
 
     is_first = side == 0
 
@@ -244,11 +250,12 @@
     near(0)
     send_totals(0)
     near(1)
-    for i in range(1, CHUNKS):
-        send_totals(i)
+    send_totals(1)
+    send_totals(2)
     near(2)
+    send_totals(3)
+    near(3)
     send_entering(0)
-    near(3)
     mixed_sums = split(wsum[...])
     read_near = dot3(mixed_sums, write, 1, 0)
     write_near = dot3(mixed_sums, read, 0, 0)
@@ -257,22 +264,24 @@
     for copy in last_copies:
         copy.wait()
 
+    state_b = split(jnp.concatenate([fs[0, 1], fs[1, 1]], axis=1))
     state_f = split(jnp.concatenate([fs[0, 0], fs[1, 0]], axis=1))
-    state_b = split(jnp.concatenate([fs[0, 1], fs[1, 1]], axis=1))
-    write_all = write_near + dot3(outof_s, state_b, 1, 1)
-    read_all = read_near + dot3(into_g, state_f, 1, 1)
-    for j in range(nh):
-        tot[j, :ck] = write_all[j * ck : (j + 1) * ck]
-        tot[j, ck:] = read_all[j * ck : (j + 1) * ck]
     h_copies = []
-    for k in range(1, nh):
-        peer = lax.rem(head + k, nh)
-        copy = pltpu.make_async_remote_copy(
-            tot.at[peer], rs.at[k - 1], h_send.at[k - 1], h_recv.at[k - 1],
-            device_id=(ctx, peer), device_id_type=MESH,
-        )
-        copy.start()
-        h_copies.append(copy)
+    for which, (nearby, factor, far) in enumerate((
+        (write_near, outof_s, state_b), (read_near, into_g, state_f),
+    )):
+        total = nearby + dot3(factor, far, 1, 1)
+        for j in range(nh):
+            tot[which, j] = total[j * ck : (j + 1) * ck]
+        for k in range(1, nh):
+            peer = lax.rem(head + k, nh)
+            copy = pltpu.make_async_remote_copy(
+                tot.at[which, peer], rs.at[which, k - 1],
+                h_send.at[which, k - 1], h_recv.at[which, k - 1],
+                device_id=(ctx, peer), device_id_type=MESH,
+            )
+            copy.start()
+            h_copies.append(copy)
 
     out_ref[...] += into_w * dot3(read, state_f, 1, 0)
     stores[0].start()
@@ -290,14 +299,13 @@
     gstep_ref[...] = steps[:heads]
     stores[2].start()
 
-    result = tot[head]
-    for k, copy in enumerate(h_copies):
-        copy.wait()
-        result = result + rs[k]
-    wg_ref[...] = result[:ck]
-    stores[3].start()
-    rg_ref[...] = result[ck:]
-    stores[4].start()
+    for which, (target, store) in enumerate(((wg_ref, stores[3]), (rg_ref, stores[4]))):
+        result = tot[which, head]
+        for k in range(1, nh):
+            h_copies[which * (nh - 1) + k - 1].wait()
+            result = result + rs[which, k - 1]
+        target[...] = result
+        store.start()
     for copy in z_copies:
         copy.wait_send()
     for store in stores:
@@ -356,15 +364,15 @@
                 pltpu.VMEM((m, state + PAD, half), F32),
                 pltpu.VMEM((2, state, half), F32),
                 pltpu.VMEM((2, 2, state, half), F32),
-                pltpu.VMEM((nh, 2 * ck, state), F32),
-                pltpu.VMEM((nh - 1, 2 * ck, state), F32),
+                pltpu.VMEM((2, nh, ck, state), F32),
+                pltpu.VMEM((2, nh - 1, ck, state), F32),
                 pltpu.VMEM((tokens, tokens), F32),
                 pltpu.VMEM((tokens, channels), F32),
                 dma((6,)), dma((5,)),
                 dma((CHUNKS,)), dma((CHUNKS,)),
                 dma((CHUNKS, m - 1)), dma((CHUNKS, m)),
                 dma((CHUNKS,)), dma((CHUNKS,)),
-                dma((nh - 1,)), dma((nh - 1,)),
+                dma((2, nh - 1)), dma((2, nh - 1)),
             ],
             compiler_params=pltpu.CompilerParams(
                 collective_id=0, has_side_effects=True, vmem_limit_bytes=GRANT

time: 27.1 us -> 26.7 us (0.985)
  Pallas kernels: 26.2 us -> 25.9 us
    pallas_call x1, Pallas kernels: 24.3 us -> 24.1 us  [shards(): pl.pallas_call(functools.partial(kernel, n, nh), out_shape=shapes, in_spe...]
where the time goes in v4:
time: 26.7 us; the launch traced here: 26.5 us
  Pallas kernels  25.9 us (97%)
  between operations  0.64 us (2%)
    pallas_call x1, Pallas kernels, shards(): pl.pallas_call(functools.partial(kernel, n, nh), out_shape=shapes, in_spe...  24.1 us
    pallas_call x1, Pallas kernels, shards(): pl.pallas_call(place, out_shape=shapes, in_specs=[hbm] * 5, out_specs=(hb...  1.84 us

profile of v4, /device:TPU:0, one launch (start us, length us, event | category | flops | bytes accessed | tf_op | source)
XLA Modules:
  0.0 26.5 jit_solution(1053950193273461332)
XLA Ops:
  0.6 24.1 %shard_map.101 = (f32[256,256]{1,0:T(8,128)}, f32[256,256]{1,0:T(8,128)}, f32[4,256]{1,0:T(4,128)}, f32[64,128]{1,0:T(8,128)}, f32[64,128]{1,0:T(8,128)}) custom-call(f32[256,256]{1,0:T(8,128)} %x_hbm.1, f32[4,256]{1,0:T(4,128)} %step_hbm.1, f32[4,256]{1,0:T(4,128)} %log_hbm.1, f32[256,128]{1,0:T(8,128)} %b_hbm.1, f32[256,128]{1,0:T(8,128)} %c_hbm.1, ...), custom_call_target="tpu_custom_call" | custom-call | tf_op jit(solution)/shard_map/pallas_call | solution.py:348
  24.7 1.8 %shard_map.102 = (f32[256,256]{1,0:T(8,128)}, f32[256,256]{1,0:T(8,128)}, f32[4,256]{1,0:T(4,128)}, f32[64,128]{1,0:T(8,128)}, f32[64,128]{1,0:T(8,128)}) custom-call(f32[256,256]{1,0:T(8,128)} %get-tuple-element.10.refs_0_, f32[256,256]{1,0:T(8,128)} %get-tuple-element.11.refs_1_, f32[4,256]{1,0:T(4,128)} %get-tuple-element.12.refs_2_, ...), custom_call_target="tpu_custom_call" | custom-call | tf_op jit(solution)/shard_map/pallas_call | solution.py:381

commit v5 on v4

--- a/solution.py
+++ b/solution.py
@@ -11,7 +11,7 @@
 F32 = jnp.float32
 BF16 = jnp.bfloat16
 PAD = 8
-GRANT = 60 * 2**20
+GRANT = 32 * 2**20
 CHUNKS = 4
 
 
@@ -39,11 +39,10 @@
 def kernel(
     n, nh,
     x_hbm, step_hbm, log_hbm, b_hbm, c_hbm, g_hbm,
-    out_hbm, gin_hbm, gstep_hbm, wg_hbm, rg_hbm,
+    out_ref, gin_ref, gstep_ref, wg_ref, rg_ref,
     x_ref, step_ref, log_ref, b_ref, c_ref, g_ref,
-    out_ref, gin_ref, gstep_ref, wg_ref, rg_ref,
     st, r1, tz, zbuf, fsend, fs, tot, rs, wsum, back,
-    in_sem, out_sem, s1_send, s1_recv, z_send, z_recv, s3_send, s3_recv, h_send, h_recv,
+    in_sem, s1_send, s1_recv, z_send, z_recv, s3_send, s3_recv, h_send, h_recv,
 ):
     tokens, channels = x_ref.shape
     heads = step_ref.shape[0]
@@ -77,14 +76,6 @@
     ]
     for load in loads:
         load.start()
-
-    stores = [
-        pltpu.make_async_copy(source, target, out_sem.at[i])
-        for i, (source, target) in enumerate((
-            (out_ref, out_hbm), (gin_ref, gin_hbm), (gstep_ref, gstep_hbm),
-            (wg_ref, wg_hbm), (rg_ref, rg_hbm),
-        ))
-    ]
 
     mid = tokens // 2
     row_ids = lax.broadcasted_iota(jnp.int32, (tokens, tokens), 0)
@@ -284,10 +275,8 @@
             h_copies.append(copy)
 
     out_ref[...] += into_w * dot3(read, state_f, 1, 0)
-    stores[0].start()
     back_all = back[...] + outof_w * dot3(write, state_b, 1, 0)
     gin_ref[...] = step_w * back_all
-    stores[1].start()
     pick_row = lax.broadcasted_iota(jnp.int32, (16, channels), 0)
     pick_col = lax.broadcasted_iota(jnp.int32, (16, channels), 1) // width
     pick = jnp.where(pick_row == pick_col, 1.0, 0.0).astype(BF16)
@@ -297,34 +286,27 @@
         pick, low, nt, preferred_element_type=F32
     )
     gstep_ref[...] = steps[:heads]
-    stores[2].start()
-
-    for which, (target, store) in enumerate(((wg_ref, stores[3]), (rg_ref, stores[4]))):
+
+    for which, target in enumerate((wg_ref, rg_ref)):
         result = tot[which, head]
         for k in range(1, nh):
             h_copies[which * (nh - 1) + k - 1].wait()
             result = result + rs[which, k - 1]
         target[...] = result
-        store.start()
     for copy in z_copies:
         copy.wait_send()
-    for store in stores:
-        store.wait()
 
 
 def place(*refs):
-    count = (len(refs) - 2) // 3
-    sources, targets, held = refs[:count], refs[count : 2 * count], refs[2 * count : 3 * count]
-    in_sem, out_sem = refs[-2:]
-    loads = [pltpu.make_async_copy(sources[i], held[i], in_sem.at[i]) for i in range(count)]
-    stores = [pltpu.make_async_copy(held[i], targets[i], out_sem.at[i]) for i in range(count)]
-    for load in loads:
-        load.start()
-    for load, store in zip(loads, stores):
-        load.wait()
-        store.start()
-    for store in stores:
-        store.wait()
+    count = len(refs) // 2
+    sems = refs[-1]
+    copies = [
+        pltpu.make_async_copy(refs[i], refs[count + i], sems.at[i]) for i in range(count)
+    ]
+    for copy in copies:
+        copy.start()
+    for copy in copies:
+        copy.wait()
 
 
 def solution(mesh):
@@ -336,6 +318,7 @@
         heads = step_size.shape[0]
         state = write_proj.shape[1]
         half, ck = channels // 2, tokens // nh
+        vmem = pl.BlockSpec(memory_space=pltpu.VMEM)
         hbm = pl.BlockSpec(memory_space=pltpu.HBM)
         dma = pltpu.SemaphoreType.DMA
         shapes = (
@@ -347,9 +330,9 @@
         )
         results = pl.pallas_call(
             functools.partial(kernel, n, nh),
-            out_shape=shapes,
+            out_shape=tuple(pltpu.VMEM(shape.shape, F32) for shape in shapes),
             in_specs=[hbm] * 6,
-            out_specs=(hbm,) * 5,
+            out_specs=(vmem,) * 5,
             scratch_shapes=[
                 pltpu.VMEM((tokens, channels), F32),
                 pltpu.VMEM((heads, tokens), F32),
@@ -357,7 +340,6 @@
                 pltpu.VMEM((tokens, state), F32),
                 pltpu.VMEM((tokens, state), F32),
                 pltpu.VMEM((tokens, channels), F32),
-                *(pltpu.VMEM(shape.shape, F32) for shape in shapes),
                 pltpu.VMEM((2, 2, state + PAD, half), F32),
                 pltpu.VMEM((2, state + PAD, half), F32),
                 pltpu.VMEM((2, state + PAD, half), F32),
@@ -368,7 +350,7 @@
                 pltpu.VMEM((2, nh - 1, ck, state), F32),
                 pltpu.VMEM((tokens, tokens), F32),
                 pltpu.VMEM((tokens, channels), F32),
-                dma((6,)), dma((5,)),
+                dma((6,)),
                 dma((CHUNKS,)), dma((CHUNKS,)),
                 dma((CHUNKS, m - 1)), dma((CHUNKS, m)),
                 dma((CHUNKS,)), dma((CHUNKS,)),
@@ -377,16 +359,16 @@
             compiler_params=pltpu.CompilerParams(
                 collective_id=0, has_side_effects=True, vmem_limit_bytes=GRANT
             ),
-        )(head_input, step_size, log_decay, write_proj, read_proj, grad_out)
+        )(*(
+            pltpu.with_memory_space_constraint(x, pltpu.HBM)
+            for x in (head_input, step_size, log_decay, write_proj, read_proj, grad_out)
+        ))
         return pl.pallas_call(
             place,
             out_shape=shapes,
-            in_specs=[hbm] * 5,
+            in_specs=[vmem] * 5,
             out_specs=(hbm,) * 5,
-            scratch_shapes=[
-                *(pltpu.VMEM(shape.shape, F32) for shape in shapes), dma((5,)), dma((5,)),
-            ],
-            compiler_params=pltpu.CompilerParams(vmem_limit_bytes=GRANT),
+            scratch_shapes=[dma((5,))],
         )(*results)
 
     return jax.shard_map(

time: 26.7 us -> 29.3 us (1.097)
  local copies, waits for them, and re-layouts: 0 us -> 3.17 us
  Pallas kernels: 25.9 us -> 25.3 us
    unnamed x0 -> x10, local copies, waits for them, and re-layouts: none -> 3.17 us
    pallas_call x2, Pallas kernels: 25.9 us -> 25.3 us  [the longest x1 23.4 us: shards(): pl.pallas_call(functools.partial(kernel, n, nh), out_shape=tuple((pltpu.V...]
where the time goes in v5:
time: 29.3 us; the launch traced here: 29.1 us
  Pallas kernels  25.3 us (86%)
  local copies, waits for them, and re-layouts  3.17 us (11%)
  between operations  0.65 us (2%)
    pallas_call x1, Pallas kernels, shards(): pl.pallas_call(functools.partial(kernel, n, nh), out_shape=tuple((pltpu.V...  23.4 us
    unnamed x10, local copies, waits for them, and re-layouts  3.17 us
    pallas_call x1, Pallas kernels, shards(): pl.pallas_call(place, out_shape=shapes, in_specs=[vmem] * 5, out_specs=(h...  1.9 us

profile of v5, /device:TPU:0, one launch (start us, length us, event | category | flops | bytes accessed | tf_op | source)
XLA Modules:
  0.0 29.1 jit_solution(7571294349255299181)
XLA Ops:
  0.6 23.4 %shard_map.101 = (f32[256,256]{1,0:T(8,128)S(1)}, f32[256,256]{1,0:T(8,128)S(1)}, f32[4,256]{1,0:T(4,128)S(1)}, f32[64,128]{1,0:T(8,128)S(1)}, f32[64,128]{1,0:T(8,128)S(1)}) custom-call(f32[256,256]{1,0:T(8,128)} %x_hbm.1, f32[4,256]{1,0:T(4,128)} %step_hbm.1, f32[4,256]{1,0:T(4,128)} %log_hbm.1, f32[256,128]{1,0:T(8,128)} %b_hbm.1, f32[256,128]{1,0:T(8,128)} %c_hbm.1, ...), custom_call_target="tpu_custom_call" | custom-call | tf_op jit(solution)/shard_map/pallas_call | solution.py:331
  24.1 0.0 copy-start
  24.1 0.7 %copy-done = f32[256,256]{1,0:T(8,128)} copy-done((f32[256,256]{1,0:T(8,128)}, f32[256,256]{1,0:T(8,128)S(1)}, u32[]{:S(2)}) %copy-start) | copy-done | bytes 262168
  24.8 0.0 copy-start.1
  24.8 0.7 %copy-done.1 = f32[256,256]{1,0:T(8,128)} copy-done((f32[256,256]{1,0:T(8,128)}, f32[256,256]{1,0:T(8,128)S(1)}, u32[]{:S(2)}) %copy-start.1) | copy-done | bytes 262168
  25.4 0.0 copy-start.2
  25.4 0.6 %copy-done.2 = f32[64,128]{1,0:T(8,128)} copy-done((f32[64,128]{1,0:T(8,128)}, f32[64,128]{1,0:T(8,128)S(1)}, u32[]{:S(2)}) %copy-start.2) | copy-done | bytes 32792
  26.1 0.0 copy-start.3
  26.1 0.6 %copy-done.3 = f32[64,128]{1,0:T(8,128)} copy-done((f32[64,128]{1,0:T(8,128)}, f32[64,128]{1,0:T(8,128)S(1)}, u32[]{:S(2)}) %copy-start.3) | copy-done | bytes 32792
  26.7 0.0 copy-start.4
  26.7 0.6 %copy-done.4 = f32[4,256]{1,0:T(4,128)} copy-done((f32[4,256]{1,0:T(4,128)}, f32[4,256]{1,0:T(4,128)S(1)}, u32[]{:S(2)}) %copy-start.4) | copy-done | bytes 4120
  27.2 1.9 %shard_map.102 = (f32[256,256]{1,0:T(8,128)}, f32[256,256]{1,0:T(8,128)}, f32[4,256]{1,0:T(4,128)}, f32[64,128]{1,0:T(8,128)}, f32[64,128]{1,0:T(8,128)}) custom-call(f32[256,256]{1,0:T(8,128)} %copy-done, f32[256,256]{1,0:T(8,128)} %copy-done.1, f32[4,256]{1,0:T(4,128)} %copy-done.4, f32[64,128]{1,0:T(8,128)} %copy-done.2, f32[64,128]{1,0:T(8,128)} %copy-done.3), custom_call_target="tpu_custom_call" | custom-call | tf_op jit(solution)/shard_map/pallas_call | solution.py:366
Async XLA Ops:
  24.1 0.7 %copy-start = (f32[256,256]{1,0:T(8,128)}, f32[256,256]{1,0:T(8,128)S(1)}, u32[]{:S(2)}) copy-start(f32[256,256]{1,0:T(8,128)S(1)} %get-tuple-element.10.refs_0_) | copy-start | bytes 786436
  24.8 0.7 %copy-start.1 = (f32[256,256]{1,0:T(8,128)}, f32[256,256]{1,0:T(8,128)S(1)}, u32[]{:S(2)}) copy-start(f32[256,256]{1,0:T(8,128)S(1)} %get-tuple-element.11.refs_1_) | copy-start | bytes 786436
  25.4 0.6 %copy-start.2 = (f32[64,128]{1,0:T(8,128)}, f32[64,128]{1,0:T(8,128)S(1)}, u32[]{:S(2)}) copy-start(f32[64,128]{1,0:T(8,128)S(1)} %get-tuple-element.13.refs_3_) | copy-start | bytes 98308
  26.1 0.6 %copy-start.3 = (f32[64,128]{1,0:T(8,128)}, f32[64,128]{1,0:T(8,128)S(1)}, u32[]{:S(2)}) copy-start(f32[64,128]{1,0:T(8,128)S(1)} %get-tuple-element.14.refs_4_) | copy-start | bytes 98308
  26.7 0.6 %copy-start.4 = (f32[4,256]{1,0:T(4,128)}, f32[4,256]{1,0:T(4,128)S(1)}, u32[]{:S(2)}) copy-start(f32[4,256]{1,0:T(4,128)S(1)} %get-tuple-element.12.refs_2_) | copy-start | bytes 12292

commit v6 on v5

--- a/solution.py
+++ b/solution.py
@@ -369,7 +369,8 @@
             in_specs=[vmem] * 5,
             out_specs=(hbm,) * 5,
             scratch_shapes=[dma((5,))],
-        )(*results)
+            compiler_params=pltpu.CompilerParams(vmem_limit_bytes=4 * 2**20),
+        )(*(pltpu.with_memory_space_constraint(x, pltpu.VMEM) for x in results))
 
     return jax.shard_map(
         shards,

time: 29.3 us -> 25.1 us (0.86)
  local copies, waits for them, and re-layouts: 3.17 us -> 0 us
  Pallas kernels: 25.3 us -> 24.3 us
    unnamed x10 -> x0, local copies, waits for them, and re-layouts: 3.17 us -> none
    pallas_call x1, Pallas kernels: 1.9 us -> 0.85 us  [shards(): pl.pallas_call(place, out_shape=shapes, in_specs=[vmem] * 5, out_specs=(h...]
where the time goes in v6:
time: 25.1 us; the launch traced here: 24.9 us
  Pallas kernels  24.3 us (97%)
  between operations  0.64 us (3%)
    pallas_call x1, Pallas kernels, shards(): pl.pallas_call(functools.partial(kernel, n, nh), out_shape=tuple((pltpu.V...  23.4 us
    pallas_call x1, Pallas kernels, shards(): pl.pallas_call(place, out_shape=shapes, in_specs=[vmem] * 5, out_specs=(h...  0.85 us

profile of v6, /device:TPU:0, one launch (start us, length us, event | category | flops | bytes accessed | tf_op | source)
XLA Modules:
  0.0 24.9 jit_solution(9572993581477822658)
XLA Ops:
  0.6 23.4 %shard_map.101 = (f32[256,256]{1,0:T(8,128)S(1)}, f32[256,256]{1,0:T(8,128)S(1)}, f32[4,256]{1,0:T(4,128)S(1)}, f32[64,128]{1,0:T(8,128)S(1)}, f32[64,128]{1,0:T(8,128)S(1)}) custom-call(f32[256,256]{1,0:T(8,128)} %x_hbm.1, f32[4,256]{1,0:T(4,128)} %step_hbm.1, f32[4,256]{1,0:T(4,128)} %log_hbm.1, f32[256,128]{1,0:T(8,128)} %b_hbm.1, f32[256,128]{1,0:T(8,128)} %c_hbm.1, ...), custom_call_target="tpu_custom_call" | custom-call | tf_op jit(solution)/shard_map/pallas_call | solution.py:331
  24.1 0.8 %shard_map.102 = (f32[256,256]{1,0:T(8,128)}, f32[256,256]{1,0:T(8,128)}, f32[4,256]{1,0:T(4,128)}, f32[64,128]{1,0:T(8,128)}, f32[64,128]{1,0:T(8,128)}) custom-call(f32[256,256]{1,0:T(8,128)S(1)} %get-tuple-element.10.refs_0_, f32[256,256]{1,0:T(8,128)S(1)} %get-tuple-element.11.refs_1_, f32[4,256]{1,0:T(4,128)S(1)} %get-tuple-element.12.refs_2_, ...), custom_call_target="tpu_custom_call" | custom-call | tf_op jit(solution)/shard_map/pallas_call | solution.py:366

commit v7 on v6

--- a/solution.py
+++ b/solution.py
@@ -41,8 +41,8 @@
     x_hbm, step_hbm, log_hbm, b_hbm, c_hbm, g_hbm,
     out_ref, gin_ref, gstep_ref, wg_ref, rg_ref,
     x_ref, step_ref, log_ref, b_ref, c_ref, g_ref,
-    st, r1, tz, zbuf, fsend, fs, tot, rs, wsum, back,
-    in_sem, s1_send, s1_recv, z_send, z_recv, s3_send, s3_recv, h_send, h_recv,
+    st, r1, tz, za, gz, zbuf, fsend, fs, tot, rs, wsum, back,
+    in_sem, s1_send, s1_recv, a_send, a_recv, z_send, z_recv, s3_send, s3_recv, h_send, h_recv,
 ):
     tokens, channels = x_ref.shape
     heads = step_ref.shape[0]
@@ -56,6 +56,8 @@
     ctx, head = lax.axis_index("ctx"), lax.axis_index("head")
     side, row = lax.rem(ctx, 2), lax.div(ctx, 2)
     partner = row * 2 + (1 - side)
+    rank, group, groups = lax.rem(row, 2), lax.div(row, 2), m // 2
+    mate = (row + 1 - 2 * rank) * 2 + side
 
     barrier = pltpu.get_barrier_semaphore()
     pl.semaphore_signal(barrier, inc=1, device_id=(partner, head), device_id_type=MESH)
@@ -190,7 +192,7 @@
             spread(jnp.where(is_first, other_decay, own_decay)),
         )
 
-    z_copies = []
+    mate_copies = []
 
     def send_totals(i):
         first_copies[i].wait()
@@ -200,30 +202,55 @@
         if i == 0:
             for d in range(2):
                 tz[d, :PAD] = decay_0[:PAD] * decay_1[:PAD]
-        for k in range(1, m):
-            peer_row = lax.rem(row + k, m)
-            direction = jnp.where(peer_row > row, 0, 1)
-            copy = pltpu.make_async_remote_copy(
-                tz.at[direction, span(i)], zbuf.at[row, span(i)],
-                z_send.at[i, k - 1], z_recv.at[i, row],
-                device_id=(peer_row * 2 + side, head), device_id_type=MESH,
-            )
-            copy.start()
-            z_copies.append(copy)
+        copy = pltpu.make_async_remote_copy(
+            tz.at[rank, span(i)], za.at[span(i)], a_send.at[i], a_recv.at[i],
+            device_id=(mate, head), device_id_type=MESH,
+        )
+        copy.start()
+        mate_copies.append(copy)
+
+    def group_copies(act):
+        for k in range(1, groups):
+            other = lax.rem(group + k, groups)
+
+            @pl.when(jnp.where(other > group, 1, 0) == rank)
+            def _():
+                for r in range(2):
+                    act(k, r, (other * 2 + r) * 2 + side)
+
+    def group_copy(i, k, r, peer):
+        return pltpu.make_async_remote_copy(
+            gz.at[span(i)], zbuf.at[group, span(i)],
+            z_send.at[i, 2 * (k - 1) + r], z_recv.at[i, group],
+            device_id=(peer, head), device_id_type=MESH,
+        )
+
+    def send_groups(i):
+        mate_copies[i].wait()
+        own_decay, mate_decay = tz[0, :PAD], za[:PAD]
+        gz[rows_of(i)] = tz[1 - rank, rows_of(i)] + spread(own_decay) * za[rows_of(i)]
+        if i == 0:
+            gz[:PAD] = own_decay * mate_decay
+        group_copies(lambda k, r, peer: group_copy(i, k, r, peer).start())
 
     last_copies = []
 
     def send_entering(i):
         def joined(j, carried):
             pltpu.make_async_remote_copy(
-                tz.at[0, span(i)], zbuf.at[j, span(i)], z_send.at[i, 0], z_recv.at[i, j],
+                gz.at[span(i)], zbuf.at[j, span(i)], z_send.at[i, 0], z_recv.at[i, j],
                 device_id=(partner, head), device_id_type=MESH,
             ).wait_recv()
             return zbuf[j, rows_of(i)] + spread(zbuf[j, :PAD]) * carried
 
         zero = jnp.zeros((piece, half), F32)
-        carry_f = lax.fori_loop(0, row, joined, zero)
-        carry_b = lax.fori_loop(0, m - 1 - row, lambda k, c: joined(m - 1 - k, c), zero)
+        carry_f = lax.fori_loop(0, group, joined, zero)
+        carry_b = lax.fori_loop(
+            0, groups - 1 - group, lambda k, c: joined(groups - 1 - k, c), zero
+        )
+        mate_part, mate_decay = za[rows_of(i)], spread(za[:PAD])
+        carry_f = jnp.where(rank == 1, mate_part + mate_decay * carry_f, carry_f)
+        carry_b = jnp.where(rank == 0, mate_part + mate_decay * carry_b, carry_b)
         part_0, part_1, decay_0, decay_1 = pair_parts(i)
         enter_f = (carry_f, decay_0 * carry_f + part_0[0])
         enter_b = (part_1[1] + decay_1 * carry_b, carry_b)
@@ -239,18 +266,23 @@
         last_copies.append(copy)
 
     near(0)
+    near(1)
     send_totals(0)
-    near(1)
     send_totals(1)
     send_totals(2)
+    send_groups(0)
+    send_totals(3)
+    send_groups(1)
     near(2)
-    send_totals(3)
+    send_groups(2)
+    send_groups(3)
+    send_entering(0)
     near(3)
-    send_entering(0)
+    send_entering(1)
     mixed_sums = split(wsum[...])
     read_near = dot3(mixed_sums, write, 1, 0)
     write_near = dot3(mixed_sums, read, 0, 0)
-    for i in range(1, CHUNKS):
+    for i in range(2, CHUNKS):
         send_entering(i)
     for copy in last_copies:
         copy.wait()
@@ -293,8 +325,8 @@
             h_copies[which * (nh - 1) + k - 1].wait()
             result = result + rs[which, k - 1]
         target[...] = result
-    for copy in z_copies:
-        copy.wait_send()
+    for i in range(CHUNKS):
+        group_copies(lambda k, r, peer: group_copy(i, k, r, peer).wait_send())
 
 
 def place(*refs):
@@ -343,7 +375,9 @@
                 pltpu.VMEM((2, 2, state + PAD, half), F32),
                 pltpu.VMEM((2, state + PAD, half), F32),
                 pltpu.VMEM((2, state + PAD, half), F32),
-                pltpu.VMEM((m, state + PAD, half), F32),
+                pltpu.VMEM((state + PAD, half), F32),
+                pltpu.VMEM((state + PAD, half), F32),
+                pltpu.VMEM((m // 2, state + PAD, half), F32),
                 pltpu.VMEM((2, state, half), F32),
                 pltpu.VMEM((2, 2, state, half), F32),
                 pltpu.VMEM((2, nh, ck, state), F32),
@@ -352,7 +386,8 @@
                 pltpu.VMEM((tokens, channels), F32),
                 dma((6,)),
                 dma((CHUNKS,)), dma((CHUNKS,)),
-                dma((CHUNKS, m - 1)), dma((CHUNKS, m)),
+                dma((CHUNKS,)), dma((CHUNKS,)),
+                dma((CHUNKS, m - 2)), dma((CHUNKS, m // 2)),
                 dma((CHUNKS,)), dma((CHUNKS,)),
                 dma((2, nh - 1)), dma((2, nh - 1)),
             ],

time: 25.1 us -> 26.7 us (1.064)
  Pallas kernels: 24.3 us -> 25.9 us
    pallas_call x1, Pallas kernels: 23.4 us -> 25.1 us  [shards(): pl.pallas_call(functools.partial(kernel, n, nh), out_shape=tuple((pltpu.V...]
where the time goes in v7:
time: 26.7 us; the launch traced here: 26.5 us
  Pallas kernels  25.9 us (97%)
  between operations  0.64 us (2%)
    pallas_call x1, Pallas kernels, shards(): pl.pallas_call(functools.partial(kernel, n, nh), out_shape=tuple((pltpu.V...  25.1 us
    pallas_call x1, Pallas kernels, shards(): pl.pallas_call(place, out_shape=shapes, in_specs=[vmem] * 5, out_specs=(h...  0.85 us

profile of v7, /device:TPU:0, one launch (start us, length us, event | category | flops | bytes accessed | tf_op | source)
XLA Modules:
  0.0 26.5 jit_solution(1341531794003179999)
XLA Ops:
  0.6 25.1 %shard_map.101 = (f32[256,256]{1,0:T(8,128)S(1)}, f32[256,256]{1,0:T(8,128)S(1)}, f32[4,256]{1,0:T(4,128)S(1)}, f32[64,128]{1,0:T(8,128)S(1)}, f32[64,128]{1,0:T(8,128)S(1)}) custom-call(f32[256,256]{1,0:T(8,128)} %x_hbm.1, f32[4,256]{1,0:T(4,128)} %step_hbm.1, f32[4,256]{1,0:T(4,128)} %log_hbm.1, f32[256,128]{1,0:T(8,128)} %b_hbm.1, f32[256,128]{1,0:T(8,128)} %c_hbm.1, ...), custom_call_target="tpu_custom_call" | custom-call | tf_op jit(solution)/shard_map/pallas_call | solution.py:363
  25.7 0.8 %shard_map.102 = (f32[256,256]{1,0:T(8,128)}, f32[256,256]{1,0:T(8,128)}, f32[4,256]{1,0:T(4,128)}, f32[64,128]{1,0:T(8,128)}, f32[64,128]{1,0:T(8,128)}) custom-call(f32[256,256]{1,0:T(8,128)S(1)} %get-tuple-element.10.refs_0_, f32[256,256]{1,0:T(8,128)S(1)} %get-tuple-element.11.refs_1_, f32[4,256]{1,0:T(4,128)S(1)} %get-tuple-element.12.refs_2_, ...), custom_call_target="tpu_custom_call" | custom-call | tf_op jit(solution)/shard_map/pallas_call | solution.py:401

commit v8 on v6

--- a/solution.py
+++ b/solution.py
@@ -12,7 +12,7 @@
 BF16 = jnp.bfloat16
 PAD = 8
 GRANT = 32 * 2**20
-CHUNKS = 4
+CHUNKS = 2
 
 
 def split(x):
@@ -21,9 +21,15 @@
 
 
 def dot3(a, b, ca, cb):
+    dims = (((ca,), (cb,)), ((), ()))
+    dot = functools.partial(lax.dot_general, dimension_numbers=dims, preferred_element_type=F32)
+    columns = b[0].shape[1 - cb]
+    if columns <= 128:
+        both = dot(a[0], jnp.concatenate([b[0], b[1]], axis=1 - cb))
+        return both[:, :columns] + (both[:, columns:] + dot(a[1], b[0]))
     left = jnp.concatenate([a[0], a[0], a[1]], axis=ca)
     right = jnp.concatenate([b[0], b[1], b[0]], axis=cb)
-    return lax.dot_general(left, right, (((ca,), (cb,)), ((), ())), preferred_element_type=F32)
+    return dot(left, right)
 
 
 def thirds(rows):
@@ -242,16 +248,13 @@
     send_totals(0)
     near(1)
     send_totals(1)
-    send_totals(2)
     near(2)
-    send_totals(3)
     near(3)
     send_entering(0)
     mixed_sums = split(wsum[...])
     read_near = dot3(mixed_sums, write, 1, 0)
     write_near = dot3(mixed_sums, read, 0, 0)
-    for i in range(1, CHUNKS):
-        send_entering(i)
+    send_entering(1)
     for copy in last_copies:
         copy.wait()
 

time: 25.1 us -> 25.3 us (level)
  no operation moved by 1% of the time
where the time goes in v8:
time: 25.3 us; the launch traced here: 25.1 us
  Pallas kernels  24.4 us (96%)
  between operations  0.64 us (3%)
    pallas_call x1, Pallas kernels, shards(): pl.pallas_call(functools.partial(kernel, n, nh), out_shape=tuple((pltpu.V...  23.6 us
    pallas_call x1, Pallas kernels, shards(): pl.pallas_call(place, out_shape=shapes, in_specs=[vmem] * 5, out_specs=(h...  0.85 us

profile of v8, /device:TPU:0, one launch (start us, length us, event | category | flops | bytes accessed | tf_op | source)
XLA Modules:
  0.0 25.1 jit_solution(2856137453152492353)
XLA Ops:
  0.6 23.6 %shard_map.101 = (f32[256,256]{1,0:T(8,128)S(1)}, f32[256,256]{1,0:T(8,128)S(1)}, f32[4,256]{1,0:T(4,128)S(1)}, f32[64,128]{1,0:T(8,128)S(1)}, f32[64,128]{1,0:T(8,128)S(1)}) custom-call(f32[256,256]{1,0:T(8,128)} %x_hbm.1, f32[4,256]{1,0:T(4,128)} %step_hbm.1, f32[4,256]{1,0:T(4,128)} %log_hbm.1, f32[256,128]{1,0:T(8,128)} %b_hbm.1, f32[256,128]{1,0:T(8,128)} %c_hbm.1, ...), custom_call_target="tpu_custom_call" | custom-call | tf_op jit(solution)/shard_map/pallas_call | solution.py:334
  24.2 0.8 %shard_map.102 = (f32[256,256]{1,0:T(8,128)}, f32[256,256]{1,0:T(8,128)}, f32[4,256]{1,0:T(4,128)}, f32[64,128]{1,0:T(8,128)}, f32[64,128]{1,0:T(8,128)}) custom-call(f32[256,256]{1,0:T(8,128)S(1)} %get-tuple-element.10.refs_0_, f32[256,256]{1,0:T(8,128)S(1)} %get-tuple-element.11.refs_1_, f32[4,256]{1,0:T(4,128)S(1)} %get-tuple-element.12.refs_2_, ...), custom_call_target="tpu_custom_call" | custom-call | tf_op jit(solution)/shard_map/pallas_call | solution.py:369

commit v9 on v8

--- a/solution.py
+++ b/solution.py
@@ -77,7 +77,7 @@
         pltpu.make_async_copy(source, target, in_sem.at[i])
         for i, (source, target) in enumerate((
             (log_hbm, log_ref), (step_hbm, step_ref), (b_hbm, b_ref),
-            (c_hbm, c_ref), (x_hbm, x_ref), (g_hbm, g_ref),
+            (x_hbm, x_ref), (c_hbm, c_ref), (g_hbm, g_ref),
         ))
     ]
     for load in loads:
@@ -114,38 +114,42 @@
 
     loads[2].wait()
     write, write_t = split(b_ref[...]), split(b_ref[...].T)
+    decay_rows = jnp.broadcast_to(into_w[tokens - 1 : tokens], (PAD, channels))
+
+    def span(i):
+        return pl.ds(0, PAD + piece) if i == 0 else pl.ds(PAD + i * piece, piece)
+
+    def spread(decay):
+        return jnp.concatenate([decay] * (piece // PAD), axis=0)
+
+    def send_first(d, whole):
+        for j in range(2):
+            st[j, d, :PAD] = decay_rows[:, j * half : (j + 1) * half]
+            st[j, d, PAD:] = whole[:, j * half : (j + 1) * half]
+        copies = [
+            pltpu.make_async_remote_copy(
+                st.at[1 - side, d, span(i)], r1.at[d, span(i)],
+                s1_send.at[d, i], s1_recv.at[d, i],
+                device_id=(partner, head), device_id_type=MESH,
+            )
+            for i in range(CHUNKS)
+        ]
+        for copy in copies:
+            copy.start()
+        return copies
+
     loads[3].wait()
-    read, read_t = split(c_ref[...]), split(c_ref[...].T)
-    loads[4].wait()
     scaled = x_ref[...] * step_w
     outof_s = split(outof_w * scaled)
     fwd = dot3(write_t, outof_s, 1, 0)
+    pl.semaphore_wait(barrier, 1 + (m - 1) + (nh - 1))
+    fwd_copies = send_first(0, fwd)
+    loads[4].wait()
+    read, read_t = split(c_ref[...]), split(c_ref[...].T)
     loads[5].wait()
     grads = g_ref[...]
     into_g = split(into_w * grads)
-    bwd = dot3(read_t, into_g, 1, 0)
-    decay_rows = jnp.broadcast_to(into_w[tokens - 1 : tokens], (PAD, channels))
-    for j in range(2):
-        for d, whole in enumerate((fwd, bwd)):
-            st[j, d, :PAD] = decay_rows[:, j * half : (j + 1) * half]
-            st[j, d, PAD:] = whole[:, j * half : (j + 1) * half]
-
-    def span(i):
-        return pl.ds(0, PAD + piece) if i == 0 else pl.ds(PAD + i * piece, piece)
-
-    def spread(decay):
-        return jnp.concatenate([decay] * (piece // PAD), axis=0)
-
-    pl.semaphore_wait(barrier, 1 + (m - 1) + (nh - 1))
-    first_copies = [
-        pltpu.make_async_remote_copy(
-            st.at[1 - side, :, span(i)], r1.at[:, span(i)], s1_send.at[i], s1_recv.at[i],
-            device_id=(partner, head), device_id_type=MESH,
-        )
-        for i in range(CHUNKS)
-    ]
-    for copy in first_copies:
-        copy.start()
+    bwd_copies = send_first(1, dot3(read_t, into_g, 1, 0))
 
     scaled_2, grads_2 = split(scaled), split(grads)
     panels = ((0, mid), (mid, tokens))
@@ -199,7 +203,8 @@
     z_copies = []
 
     def send_totals(i):
-        first_copies[i].wait()
+        fwd_copies[i].wait()
+        bwd_copies[i].wait()
         part_0, part_1, decay_0, decay_1 = pair_parts(i)
         tz[0, rows_of(i)] = decay_1 * part_0[0] + part_1[0]
         tz[1, rows_of(i)] = part_0[1] + decay_0 * part_1[1]
@@ -354,7 +359,7 @@
                 pltpu.VMEM((tokens, tokens), F32),
                 pltpu.VMEM((tokens, channels), F32),
                 dma((6,)),
-                dma((CHUNKS,)), dma((CHUNKS,)),
+                dma((2, CHUNKS)), dma((2, CHUNKS)),
                 dma((CHUNKS, m - 1)), dma((CHUNKS, m)),
                 dma((CHUNKS,)), dma((CHUNKS,)),
                 dma((2, nh - 1)), dma((2, nh - 1)),

time: 25.3 us -> 25.4 us (level)
  no operation moved by 1% of the time
where the time goes in v9:
time: 25.4 us; the launch traced here: 25.2 us
  Pallas kernels  24.6 us (97%)
  between operations  0.64 us (3%)
    pallas_call x1, Pallas kernels, shards(): pl.pallas_call(functools.partial(kernel, n, nh), out_shape=tuple((pltpu.V...  23.7 us
    pallas_call x1, Pallas kernels, shards(): pl.pallas_call(place, out_shape=shapes, in_specs=[vmem] * 5, out_specs=(h...  0.85 us

profile of v9, /device:TPU:0, one launch (start us, length us, event | category | flops | bytes accessed | tf_op | source)
XLA Modules:
  0.0 25.2 jit_solution(4593385885382071010)
XLA Ops:
  0.6 23.7 %shard_map.101 = (f32[256,256]{1,0:T(8,128)S(1)}, f32[256,256]{1,0:T(8,128)S(1)}, f32[4,256]{1,0:T(4,128)S(1)}, f32[64,128]{1,0:T(8,128)S(1)}, f32[64,128]{1,0:T(8,128)S(1)}) custom-call(f32[256,256]{1,0:T(8,128)} %x_hbm.1, f32[4,256]{1,0:T(4,128)} %step_hbm.1, f32[4,256]{1,0:T(4,128)} %log_hbm.1, f32[256,128]{1,0:T(8,128)} %b_hbm.1, f32[256,128]{1,0:T(8,128)} %c_hbm.1, ...), custom_call_target="tpu_custom_call" | custom-call | tf_op jit(solution)/shard_map/pallas_call | solution.py:339
  24.4 0.8 %shard_map.102 = (f32[256,256]{1,0:T(8,128)}, f32[256,256]{1,0:T(8,128)}, f32[4,256]{1,0:T(4,128)}, f32[64,128]{1,0:T(8,128)}, f32[64,128]{1,0:T(8,128)}) custom-call(f32[256,256]{1,0:T(8,128)S(1)} %get-tuple-element.10.refs_0_, f32[256,256]{1,0:T(8,128)S(1)} %get-tuple-element.11.refs_1_, f32[4,256]{1,0:T(4,128)S(1)} %get-tuple-element.12.refs_2_, ...), custom_call_target="tpu_custom_call" | custom-call | tf_op jit(solution)/shard_map/pallas_call | solution.py:374
